TPU v7x, 256 devices: a whole 4x4x8 slice. The times are simulated.
256 devices in a mesh: gx: 32 (over x, z), gy: 8 (over y, core).
Axes of the slice: x: 4, y: 4, z: 8, core: 2. Of those that a mesh axis runs over, the one named last changes fastest.
Arguments:
- displacement: float32 [3, 256, 128, 128], P(None, 'gx', 'gy'), may hold values from -6 to 6
- velocity: float32 [3, 256, 128, 128], P(None, 'gx', 'gy'), may hold values from -3 to 3
- plastic: float32 [30, 256, 128, 128], P(None, 'gx', 'gy'), may hold values from -1.2 to 1.2
- lumped_mass: float32 [256, 128, 128], P('gx', 'gy'), may hold values from 1 to 4
- material: int32 [256, 128, 128], P('gx', 'gy'), may hold values from 0 to 7
- moduli: float32 [8, 6], replicated, may hold values from 0.05 to 0.4
- yield_radii: float32 [8, 5], replicated, may hold values from 0.02 to 0.6
- history: float32 [1024, 21, 3072], P('gx', None, 'gy'), may hold values from -6 to 6
- drm_coef: float32 [1024, 2, 3072], P('gx', None, 'gy'), may hold values from 0.3 to 3
- layer_nodes: int32 [32, 98304], P('gx', 'gy'), may hold values from 0 to 16384, as said below
Outputs:
- final_displacement: float32 [3, 256, 128, 128], P(None, 'gx', 'gy')
- final_plastic: float32 [30, 256, 128, 128], P(None, 'gx', 'gy')
Inputs may be any that keep to these rules, and one draw needn't show every extreme that they name: `layer_nodes`: entries are flat indices over (8, 16, 128) of a block's nodes, or 16384 for an empty slot; live entries of one block are distinct; the blocks at both ends along gx have all 12288 slots live, the others a quarter to a half of them.
All inputs are finite; a program needn't handle non-finite values.
Results may differ from a plain program's by a relative error of at most 0.0003.
Values sent between devices are 32-bit elements; how exact they have to be, the bound alone decides.
A program may use at most 128 MiB of HBM per device.

v0:
```python
import math

import jax
import jax.numpy as jnp
from jax import lax
from jax.sharding import PartitionSpec as P

STEPS = 5


time_step = 0.7


def from_behind(block, axis, distance):
    devices = range(lax.axis_size(axis))
    route = [(i - distance, i) for i in devices if i - distance in devices]
    return lax.ppermute(block, axis, route)


def corner(extended, near_x, near_y, near_z):
    return extended[
        :,
        near_x : near_x + extended.shape[1] - 1,
        near_y : near_y + extended.shape[2] - 1,
        near_z : near_z + extended.shape[3] - 1,
    ]


def material_props(material, moduli, yield_radii):
    soil_table = jnp.concatenate([moduli, yield_radii], axis=1)
    levels = jnp.arange(soil_table.shape[0], dtype=jnp.int32)
    onehot = (material[None] == levels[:, None, None, None]).astype(jnp.float32)
    return jnp.einsum("mxyz,mp->pxyz", onehot, soil_table, precision=lax.Precision.HIGHEST)


def drm_force(before, middle, after, coef_mass, coef_stiff):
    return coef_mass * (after - 2.0 * middle + before) + coef_stiff * middle


def drm_steps(stored, coefs):
    readers = stored.shape[0]
    piece_len = stored.shape[2]
    levels = stored.reshape(readers, 3, STEPS + 2, piece_len)
    coef_mass = coefs[:, 0:1]
    coef_stiff = coefs[:, 1:2]
    outputs = [
        drm_force(
            levels[:, :, step_index],
            levels[:, :, step_index + 1],
            levels[:, :, step_index + 2],
            coef_mass,
            coef_stiff,
        )
        for step_index in range(STEPS)
    ]
    return jnp.stack(outputs, axis=1)


def place_forces(slot_values, node_index, cells_x, cells_y, cells_z):
    rows = slot_values.shape[0]
    slots = slot_values.shape[1]
    columns = cells_x * cells_y
    block = math.gcd(slots, 2048)
    turns = slots // block
    value_blocks = jnp.transpose(slot_values.reshape(rows, turns, block), (1, 2, 0))
    index_blocks = node_index.reshape(turns, block)
    column_ids = jnp.arange(columns, dtype=jnp.int32)
    depth_ids = jnp.arange(cells_z, dtype=jnp.int32)

    def add_block(total, pieces):
        values, indices = pieces
        column_hot = (indices[:, None] // cells_z == column_ids[None, :]).astype(jnp.float32)
        depth_hot = (indices[:, None] % cells_z == depth_ids[None, :]).astype(jnp.float32)
        spread = (values[:, :, None] * depth_hot[:, None, :]).reshape(block, rows * cells_z)
        placed = lax.dot_general(
            column_hot,
            spread,
            (((0,), (0,)), ((), ())),
            precision=lax.Precision.HIGHEST,
            preferred_element_type=jnp.float32,
        )
        return (total + placed, None)

    start = jnp.zeros((columns, rows * cells_z), jnp.float32)
    total, unused = lax.scan(add_block, start, (value_blocks, index_blocks))
    placed = jnp.transpose(total.reshape(columns, rows, cells_z), (1, 0, 2))
    return placed.reshape(rows, cells_x, cells_y, cells_z)


def element_forces(extended, plastic, material_data):
    grad_x = 0.0
    grad_y = 0.0
    grad_z = 0.0
    for near_y in (0, 1):
        for near_z in (0, 1):
            grad_x = (
                grad_x + corner(extended, 1, near_y, near_z) - corner(extended, 0, near_y, near_z)
            )
    for near_x in (0, 1):
        for near_z in (0, 1):
            grad_y = (
                grad_y + corner(extended, near_x, 1, near_z) - corner(extended, near_x, 0, near_z)
            )
    for near_x in (0, 1):
        for near_y in (0, 1):
            grad_z = (
                grad_z + corner(extended, near_x, near_y, 1) - corner(extended, near_x, near_y, 0)
            )
    grad_x = 0.25 * grad_x
    grad_y = 0.25 * grad_y
    grad_z = 0.25 * grad_z
    strain_xx = grad_x[0]
    strain_yy = grad_y[1]
    strain_zz = grad_z[2]
    strain_xy = 0.5 * (grad_y[0] + grad_x[1])
    strain_yz = 0.5 * (grad_z[1] + grad_y[2])
    strain_zx = 0.5 * (grad_x[2] + grad_z[0])
    volume_strain = strain_xx + strain_yy + strain_zz
    mean_strain = volume_strain / 3.0
    deviator = [
        strain_xx - mean_strain,
        strain_yy - mean_strain,
        strain_zz - mean_strain,
        strain_xy,
        strain_yz,
        strain_zx,
    ]
    surfaces = (material_data.shape[0] - 1) // 2
    deviator_sum = [jnp.zeros_like(strain_xx) for comp in range(6)]
    new_plastic = []
    for surface in range(surfaces):
        shear_mod = material_data[1 + surface]
        radius = material_data[1 + surfaces + surface]
        trial = [
            2.0 * shear_mod * (deviator[comp] - plastic[6 * surface + comp]) for comp in range(6)
        ]
        sq_norm = (
            trial[0] * trial[0]
            + trial[1] * trial[1]
            + trial[2] * trial[2]
            + 2.0 * (trial[3] * trial[3] + trial[4] * trial[4] + trial[5] * trial[5])
        )
        radius_sq = radius * radius
        factor = jnp.sqrt(radius_sq / jnp.maximum(sq_norm, radius_sq))
        for comp in range(6):
            stress_part = factor * trial[comp]
            new_plastic.append(deviator[comp] - stress_part / (2.0 * shear_mod))
            deviator_sum[comp] = deviator_sum[comp] + stress_part
    bulk_mod = material_data[0]
    pressure = bulk_mod * volume_strain
    stress_xx = deviator_sum[0] + pressure
    stress_yy = deviator_sum[1] + pressure
    stress_zz = deviator_sum[2] + pressure
    stress_xy = deviator_sum[3]
    stress_yz = deviator_sum[4]
    stress_zx = deviator_sum[5]
    column_x = 0.25 * jnp.stack([stress_xx, stress_xy, stress_zx])
    column_y = 0.25 * jnp.stack([stress_xy, stress_yy, stress_yz])
    column_z = 0.25 * jnp.stack([stress_zx, stress_yz, stress_zz])
    force_ext = 0.0
    for near_x in (0, 1):
        for near_y in (0, 1):
            for near_z in (0, 1):
                corner_force = (
                    (2 * near_x - 1) * column_x
                    + (2 * near_y - 1) * column_y
                    + (2 * near_z - 1) * column_z
                )
                force_ext = force_ext + jnp.pad(
                    corner_force,
                    ((0, 0), (near_x, 1 - near_x), (near_y, 1 - near_y), (near_z, 1 - near_z)),
                )
    return (force_ext, jnp.stack(new_plastic))


def extend_nodes(current):
    x_face = from_behind(current[:, 0:1], "gx", -1)
    x_wide = jnp.concatenate([current, x_face], axis=1)
    y_row = from_behind(x_wide[:, :, 0:1], "gy", -1)
    extended = jnp.concatenate([x_wide, y_row], axis=2)
    return jnp.pad(extended, ((0, 0), (0, 0), (0, 0), (0, 1)))


def fold_forces(force_ext, cells_x, cells_y, cells_z):
    owned_part = force_ext[:, :, :cells_y, :cells_z]
    y_row = from_behind(force_ext[:, :, cells_y : cells_y + 1, :cells_z], "gy", 1)
    owned_part = owned_part.at[:, :, 0:1].add(y_row)
    x_face = from_behind(owned_part[:, cells_x : cells_x + 1], "gx", 1)
    interior = owned_part[:, :cells_x]
    return interior.at[:, 0:1].add(x_face)


def per_device(
    displacement,
    velocity,
    plastic,
    lumped_mass,
    material,
    moduli,
    yield_radii,
    history,
    drm_coef,
    layer_nodes,
):
    cells_x = displacement.shape[1]
    cells_y = displacement.shape[2]
    cells_z = displacement.shape[3]
    arrived, coefs = (
        lax.all_to_all(history, "gx", split_axis=0, concat_axis=0, tiled=True),
        lax.all_to_all(drm_coef, "gx", split_axis=0, concat_axis=0, tiled=True),
    )
    drm_terms = drm_steps(arrived, coefs)
    slot_values = jnp.transpose(drm_terms, (1, 2, 0, 3)).reshape(STEPS * 3, -1)
    node_index = layer_nodes.reshape(-1)
    all_nodes = place_forces(slot_values, node_index, cells_x, cells_y, cells_z).reshape(
        STEPS, 3, cells_x, cells_y, cells_z
    )
    material_data = material_props(material, moduli, yield_radii)
    previous = displacement - time_step * velocity
    current = displacement
    for step_index in range(STEPS):
        extended = extend_nodes(current)
        force_ext, plastic = element_forces(extended, plastic, material_data)
        internal = fold_forces(force_ext, cells_x, cells_y, cells_z)
        upcoming = (
            2.0 * current
            - previous
            + time_step * time_step * (all_nodes[step_index] - internal) / lumped_mass[None]
        )
        previous = current
        current = upcoming
    return (current, plastic)


def solution(mesh):
    return jax.shard_map(
        per_device,
        mesh=mesh,
        in_specs=(
            P(None, "gx", "gy", None),
            P(None, "gx", "gy", None),
            P(None, "gx", "gy", None),
            P("gx", "gy", None),
            P("gx", "gy", None),
            P(),
            P(),
            P("gx", None, "gy"),
            P("gx", None, "gy"),
            P("gx", "gy"),
        ),
        out_specs=(P(None, "gx", "gy", None), P(None, "gx", "gy", None)),
        check_vma=False,
    )
```

profile of v0, /device:TPU:3, one launch (start us, length us, event | category | flops | bytes accessed | tf_op | source)
XLA Modules:
  0.0 320.3 jit_solution(12622225786719873390)
XLA Ops:
  0.6 11.1 %all-to-all-start = ((f32[32,2,384]{2,1,0:T(2,128)}), f32[32,2,384]{2,1,0:T(2,128)}, u32[]{:S(2)}, u32[]{:S(2)}) async-start(f32[32,2,384]{2,1,0:T(2,128)} %param.40), calls=%async_computation | async-start | bytes 196608 | tf_op jit(solution)/shard_map/all_to_all | solution.py:210
  12.6 4.3 %collective-permute-start = (f32[3,1,16,128]{3,2,1,0:T(8,128)S(1)}, f32[3,1,16,128]{3,2,1,0:T(8,128)S(1)}, u32[]{:S(2)}, u32[]{:S(2)}) collective-permute-start(f32[3,1,16,128]{3,2,1,0:T(8,128)S(1)} %slice.979), channel_id=1, source_target_pairs={{8,0},{16,8},{24,16},{32,24},{40,32},{48,40},{56,48},{64,56},{72,6... | collective-permute-start | bytes 73736 | tf_op jit(solution)/shard_map/ppermute | solution.py:17
  19.5 3.6 %collective-permute-start.1 = (f32[3,9,1,128]{3,2,1,0:T(1,128)S(1)}, f32[3,9,1,128]{3,2,1,0:T(1,128)S(1)}, u32[]{:S(2)}, u32[]{:S(2)}) collective-permute-start(f32[3,9,1,128]{3,2,1,0:T(1,128)S(1)} %slice.1155), channel_id=1, source_target_pairs={{1,0},{2,1},{3,2},{4,3},{5,4},{6,5},{7,6},{9,8},{10,9},{11,10},{12... | collective-permute-start | bytes 41480 | tf_op jit(solution)/shard_map/ppermute | solution.py:17
  28.3 7.9 %all-to-all-start.1 = ((f32[32,21,384]{2,1,0:T(8,128)}), f32[32,21,384]{2,1,0:T(8,128)}, u32[]{:S(2)}, u32[]{:S(2)}) async-start(f32[32,21,384]{2,1,0:T(8,128)} %copy.232), calls=%async_computation.1 | async-start | bytes 2359296 | tf_op jit(solution)/shard_map/all_to_all | solution.py:209
  38.1 3.3 %collective-permute-start.2 = (f32[3,9,1,128]{3,2,1,0:T(1,128)S(1)}, f32[3,9,1,128]{3,2,1,0:T(1,128)S(1)}, u32[]{:S(2)}, u32[]{:S(2)}) collective-permute-start(f32[3,9,1,128]{3,2,1,0:T(1,128)S(1)} %slice.1180), channel_id=1, source_target_pairs={{0,1},{1,2},{2,3},{3,4},{4,5},{5,6},{6,7},{8,9},{9,10},{10,11},{11... | collective-permute-start | bytes 41480 | tf_op jit(solution)/shard_map/ppermute | solution.py:17
  43.0 3.3 %collective-permute-start.3 = (f32[3,1,16,128]{3,2,1,0:T(8,128)}, f32[3,1,16,128]{3,2,1,0:T(8,128)}, u32[]{:S(2)}, u32[]{:S(2)}) collective-permute-start(f32[3,1,16,128]{3,2,1,0:T(8,128)} %slice.1183), channel_id=1, source_target_pairs={{0,8},{8,16},{16,24},{24,32},{32,40},{40,48},{48,56},{56,64},{64,7... | collective-permute-start | bytes 73736 | tf_op jit(solution)/shard_map/ppermute | solution.py:17
  46.8 2.2 reduce.23
  52.0 13.2 %collective-permute-done.3 = f32[3,1,16,128]{3,2,1,0:T(8,128)} collective-permute-done((f32[3,1,16,128]{3,2,1,0:T(8,128)}, f32[3,1,16,128]{3,2,1,0:T(8,128)}, u32[]{:S(2)}, u32[]{:S(2)}) %collective-permute-start.3) | collective-permute-done | bytes 24608 | tf_op jit(solution)/shard_map/ppermute | solution.py:17
  70.9 2.2 reshape_reshape.8
  73.1 132.0 %while.25 = (s32[]{:T(128)}, f32[128,1920]{1,0:T(8,128)S(1)}, s32[6,2048]{1,0:T(8,128)}, f32[6,2048,15]{1,0,2:T(8,128)}, s32[]{:T(128)}, /*index=5*/s32[]{:T(128)}) while((s32[]{:T(128)}, f32[128,1920]{1,0:T(8,128)S(1)}, s32[6,2048]{1,0:T(8,128)}, f32[6,2048,15]{1,0,2:T(8,128)}, s32[]{:T(128)}, ...), condition=%wide.region_1.2_spmd.clone.clone, body=%wide.region_0.1_spmd.clone.clone.sunk | while | flops 6045046784 | bytes 36192348 | solution.py:85
  75.5 7.5 %broadcast_multiply_fusion.7 = f32[2048,15,128]{0,2,1:T(8,128)} fusion(f32[2048,128]{0,1:T(8,128)S(1)} %fusion.118, f32[2048,15]{0,1:T(8,128)S(1)} %bitcast.193), kind=kLoop, calls=%fused_computation.1.clone.1 | loop fusion | flops 3932160 | bytes 16900096 | tf_op jit(solution)/shard_map/while/body/eval_jaxpr/mul | solution.py:74
  82.9 12.2 %convolution_add_fusion.2 = f32[128,1920]{1,0:T(8,128)S(1)} fusion(f32[2048,1920]{0,1:T(8,128)} %bitcast.117, f32[128,1920]{1,0:T(8,128)S(1)} %get-tuple-element.594, s32[2048]{0:T(1024)S(1)} %get-tuple-element.586, pred[]{:T(512)S(6)} %compare.114), kind=kOutput, calls=%fused_computation.2.clone.1 | convolution fusion | flops 6040551424 | bytes 17702912 | tf_op jit(solution)/shard_map/while/body/eval_jaxpr/dot_general | solution.py:75
  97.5 7.5 %broadcast_multiply_fusion.7 = f32[2048,15,128]{0,2,1:T(8,128)} fusion(f32[2048,128]{0,1:T(8,128)S(1)} %fusion.118, f32[2048,15]{0,1:T(8,128)S(1)} %bitcast.193), kind=kLoop, calls=%fused_computation.1.clone.1 | loop fusion | flops 3932160 | bytes 16900096 | tf_op jit(solution)/shard_map/while/body/eval_jaxpr/mul | solution.py:74
  104.9 12.1 %convolution_add_fusion.2 = f32[128,1920]{1,0:T(8,128)S(1)} fusion(f32[2048,1920]{0,1:T(8,128)} %bitcast.117, f32[128,1920]{1,0:T(8,128)S(1)} %get-tuple-element.594, s32[2048]{0:T(1024)S(1)} %get-tuple-element.586, pred[]{:T(512)S(6)} %compare.114), kind=kOutput, calls=%fused_computation.2.clone.1 | convolution fusion | flops 6040551424 | bytes 17702912 | tf_op jit(solution)/shard_map/while/body/eval_jaxpr/dot_general | solution.py:75
  119.5 7.5 %broadcast_multiply_fusion.7 = f32[2048,15,128]{0,2,1:T(8,128)} fusion(f32[2048,128]{0,1:T(8,128)S(1)} %fusion.118, f32[2048,15]{0,1:T(8,128)S(1)} %bitcast.193), kind=kLoop, calls=%fused_computation.1.clone.1 | loop fusion | flops 3932160 | bytes 16900096 | tf_op jit(solution)/shard_map/while/body/eval_jaxpr/mul | solution.py:74
  126.9 12.1 %convolution_add_fusion.2 = f32[128,1920]{1,0:T(8,128)S(1)} fusion(f32[2048,1920]{0,1:T(8,128)} %bitcast.117, f32[128,1920]{1,0:T(8,128)S(1)} %get-tuple-element.594, s32[2048]{0:T(1024)S(1)} %get-tuple-element.586, pred[]{:T(512)S(6)} %compare.114), kind=kOutput, calls=%fused_computation.2.clone.1 | convolution fusion | flops 6040551424 | bytes 17702912 | tf_op jit(solution)/shard_map/while/body/eval_jaxpr/dot_general | solution.py:75
  141.5 7.5 %broadcast_multiply_fusion.7 = f32[2048,15,128]{0,2,1:T(8,128)} fusion(f32[2048,128]{0,1:T(8,128)S(1)} %fusion.118, f32[2048,15]{0,1:T(8,128)S(1)} %bitcast.193), kind=kLoop, calls=%fused_computation.1.clone.1 | loop fusion | flops 3932160 | bytes 16900096 | tf_op jit(solution)/shard_map/while/body/eval_jaxpr/mul | solution.py:74
  148.9 12.1 %convolution_add_fusion.2 = f32[128,1920]{1,0:T(8,128)S(1)} fusion(f32[2048,1920]{0,1:T(8,128)} %bitcast.117, f32[128,1920]{1,0:T(8,128)S(1)} %get-tuple-element.594, s32[2048]{0:T(1024)S(1)} %get-tuple-element.586, pred[]{:T(512)S(6)} %compare.114), kind=kOutput, calls=%fused_computation.2.clone.1 | convolution fusion | flops 6040551424 | bytes 17702912 | tf_op jit(solution)/shard_map/while/body/eval_jaxpr/dot_general | solution.py:75
  163.4 7.5 %broadcast_multiply_fusion.7 = f32[2048,15,128]{0,2,1:T(8,128)} fusion(f32[2048,128]{0,1:T(8,128)S(1)} %fusion.118, f32[2048,15]{0,1:T(8,128)S(1)} %bitcast.193), kind=kLoop, calls=%fused_computation.1.clone.1 | loop fusion | flops 3932160 | bytes 16900096 | tf_op jit(solution)/shard_map/while/body/eval_jaxpr/mul | solution.py:74
  170.9 12.1 %convolution_add_fusion.2 = f32[128,1920]{1,0:T(8,128)S(1)} fusion(f32[2048,1920]{0,1:T(8,128)} %bitcast.117, f32[128,1920]{1,0:T(8,128)S(1)} %get-tuple-element.594, s32[2048]{0:T(1024)S(1)} %get-tuple-element.586, pred[]{:T(512)S(6)} %compare.114), kind=kOutput, calls=%fused_computation.2.clone.1 | convolution fusion | flops 6040551424 | bytes 17702912 | tf_op jit(solution)/shard_map/while/body/eval_jaxpr/dot_general | solution.py:75
  185.4 7.5 %broadcast_multiply_fusion.7 = f32[2048,15,128]{0,2,1:T(8,128)} fusion(f32[2048,128]{0,1:T(8,128)S(1)} %fusion.118, f32[2048,15]{0,1:T(8,128)S(1)} %bitcast.193), kind=kLoop, calls=%fused_computation.1.clone.1 | loop fusion | flops 3932160 | bytes 16900096 | tf_op jit(solution)/shard_map/while/body/eval_jaxpr/mul | solution.py:74
  192.9 12.1 %convolution_add_fusion.2 = f32[128,1920]{1,0:T(8,128)S(1)} fusion(f32[2048,1920]{0,1:T(8,128)} %bitcast.117, f32[128,1920]{1,0:T(8,128)S(1)} %get-tuple-element.594, s32[2048]{0:T(1024)S(1)} %get-tuple-element.586, pred[]{:T(512)S(6)} %compare.114), kind=kOutput, calls=%fused_computation.2.clone.1 | convolution fusion | flops 6040551424 | bytes 17702912 | tf_op jit(solution)/shard_map/while/body/eval_jaxpr/dot_general | solution.py:75
  206.4 2.2 fusion.112
  209.8 2.7 collective-permute-start.4
  214.4 3.4 %collective-permute-start.5 = (f32[3,9,1,128]{3,2,1,0:T(1,128)S(1)}, f32[3,9,1,128]{3,2,1,0:T(1,128)S(1)}, u32[]{:S(2)}, u32[]{:S(2)}) collective-permute-start(f32[3,9,1,128]{3,2,1,0:T(1,128)S(1)} %pad_maximum_fusion.23), channel_id=1, source_target_pairs={{1,0},{2,1},{3,2},{4,3},{5,4},{6,5},{7,6},{9,8},{10,9},{11,10},{12... | collective-permute-start | bytes 41480 | tf_op jit(solution)/shard_map/ppermute | solution.py:17
  217.8 3.1 collective-permute-done.5
  221.7 2.9 add_add_fusion.26
  226.7 1.9 collective-permute-start.6
  232.4 4.2 %collective-permute-done.7 = f32[3,1,16,128]{3,2,1,0:T(8,128)S(1)} collective-permute-done((f32[3,1,16,128]{3,2,1,0:T(8,128)S(1)}, f32[3,1,16,128]{3,2,1,0:T(8,128)S(1)}, u32[]{:S(2)}, u32[]{:S(2)}) %collective-permute-start.7) | collective-permute-done | bytes 24608 | tf_op jit(solution)/shard_map/ppermute | solution.py:17
  236.7 2.6 collective-permute-start.8
  239.3 2.1 collective-permute-done.8
  241.4 4.6 %collective-permute-start.9 = (f32[3,9,1,128]{3,2,1,0:T(1,128)S(1)}, f32[3,9,1,128]{3,2,1,0:T(1,128)S(1)}, u32[]{:S(2)}, u32[]{:S(2)}) collective-permute-start(f32[3,9,1,128]{3,2,1,0:T(1,128)S(1)} %pad_maximum_fusion.22), channel_id=1, source_target_pairs={{1,0},{2,1},{3,2},{4,3},{5,4},{6,5},{7,6},{9,8},{10,9},{11,10},{12... | collective-permute-start | bytes 41480 | tf_op jit(solution)/shard_map/ppermute | solution.py:17
  246.0 3.0 collective-permute-done.9
  250.1 2.8 add_add_fusion.19
  254.7 1.9 collective-permute-start.10
  260.4 4.3 %collective-permute-done.11 = f32[3,1,16,128]{3,2,1,0:T(8,128)S(1)} collective-permute-done((f32[3,1,16,128]{3,2,1,0:T(8,128)S(1)}, f32[3,1,16,128]{3,2,1,0:T(8,128)S(1)}, u32[]{:S(2)}, u32[]{:S(2)}) %collective-permute-start.11) | collective-permute-done | bytes 24608 | tf_op jit(solution)/shard_map/ppermute | solution.py:17
  264.7 2.5 collective-permute-start.12
  267.2 2.1 collective-permute-done.12
  269.3 4.4 %collective-permute-start.13 = (f32[3,9,1,128]{3,2,1,0:T(1,128)S(1)}, f32[3,9,1,128]{3,2,1,0:T(1,128)S(1)}, u32[]{:S(2)}, u32[]{:S(2)}) collective-permute-start(f32[3,9,1,128]{3,2,1,0:T(1,128)S(1)} %pad_maximum_fusion.21), channel_id=1, source_target_pairs={{1,0},{2,1},{3,2},{4,3},{5,4},{6,5},{7,6},{9,8},{10,9},{11,10},{12... | collective-permute-start | bytes 41480 | tf_op jit(solution)/shard_map/ppermute | solution.py:17
  273.7 3.2 collective-permute-done.13
  281.7 1.9 collective-permute-start.14
  287.0 4.5 %collective-permute-done.15 = f32[3,1,16,128]{3,2,1,0:T(8,128)S(1)} collective-permute-done((f32[3,1,16,128]{3,2,1,0:T(8,128)S(1)}, f32[3,1,16,128]{3,2,1,0:T(8,128)S(1)}, u32[]{:S(2)}, u32[]{:S(2)}) %collective-permute-start.15) | collective-permute-done | bytes 24608 | tf_op jit(solution)/shard_map/ppermute | solution.py:17
  291.6 2.5 collective-permute-start.16
  294.1 2.1 collective-permute-done.16
  296.2 4.4 %collective-permute-start.17 = (f32[3,9,1,128]{3,2,1,0:T(1,128)S(1)}, f32[3,9,1,128]{3,2,1,0:T(1,128)S(1)}, u32[]{:S(2)}, u32[]{:S(2)}) collective-permute-start(f32[3,9,1,128]{3,2,1,0:T(1,128)S(1)} %pad_maximum_fusion.20), channel_id=1, source_target_pairs={{1,0},{2,1},{3,2},{4,3},{5,4},{6,5},{7,6},{9,8},{10,9},{11,10},{12... | collective-permute-start | bytes 41480 | tf_op jit(solution)/shard_map/ppermute | solution.py:17
  300.6 3.2 collective-permute-done.17
  309.7 1.9 collective-permute-start.18
  315.5 4.1 %collective-permute-done.19 = f32[3,1,16,128]{3,2,1,0:T(8,128)S(1)} collective-permute-done((f32[3,1,16,128]{3,2,1,0:T(8,128)S(1)}, f32[3,1,16,128]{3,2,1,0:T(8,128)S(1)}, u32[]{:S(2)}, u32[]{:S(2)}) %collective-permute-start.19) | collective-permute-done | bytes 24608 | tf_op jit(solution)/shard_map/ppermute | solution.py:17
  (631 shorter events, 68.5 us)
Async XLA Ops:
  0.6 27.6 %all-to-all-start = ((f32[32,2,384]{2,1,0:T(2,128)}), f32[32,2,384]{2,1,0:T(2,128)}, u32[]{:S(2)}, u32[]{:S(2)}) async-start(f32[32,2,384]{2,1,0:T(2,128)} %param.40), calls=%async_computation | async-start | bytes 196608 | tf_op jit(solution)/shard_map/all_to_all | solution.py:210
  12.6 6.8 %collective-permute-start = (f32[3,1,16,128]{3,2,1,0:T(8,128)S(1)}, f32[3,1,16,128]{3,2,1,0:T(8,128)S(1)}, u32[]{:S(2)}, u32[]{:S(2)}) collective-permute-start(f32[3,1,16,128]{3,2,1,0:T(8,128)S(1)} %slice.979), channel_id=1, source_target_pairs={{8,0},{16,8},{24,16},{32,24},{40,32},{48,40},{56,48},{64,56},{72,6... | collective-permute-start | bytes 73736 | tf_op jit(solution)/shard_map/ppermute | solution.py:17
  19.5 6.1 %collective-permute-start.1 = (f32[3,9,1,128]{3,2,1,0:T(1,128)S(1)}, f32[3,9,1,128]{3,2,1,0:T(1,128)S(1)}, u32[]{:S(2)}, u32[]{:S(2)}) collective-permute-start(f32[3,9,1,128]{3,2,1,0:T(1,128)S(1)} %slice.1155), channel_id=1, source_target_pairs={{1,0},{2,1},{3,2},{4,3},{5,4},{6,5},{7,6},{9,8},{10,9},{11,10},{12... | collective-permute-start | bytes 41480 | tf_op jit(solution)/shard_map/ppermute | solution.py:17
  28.3 40.0 %all-to-all-start.1 = ((f32[32,21,384]{2,1,0:T(8,128)}), f32[32,21,384]{2,1,0:T(8,128)}, u32[]{:S(2)}, u32[]{:S(2)}) async-start(f32[32,21,384]{2,1,0:T(8,128)} %copy.232), calls=%async_computation.1 | async-start | bytes 2359296 | tf_op jit(solution)/shard_map/all_to_all | solution.py:209
  38.1 4.2 %collective-permute-start.2 = (f32[3,9,1,128]{3,2,1,0:T(1,128)S(1)}, f32[3,9,1,128]{3,2,1,0:T(1,128)S(1)}, u32[]{:S(2)}, u32[]{:S(2)}) collective-permute-start(f32[3,9,1,128]{3,2,1,0:T(1,128)S(1)} %slice.1180), channel_id=1, source_target_pairs={{0,1},{1,2},{2,3},{3,4},{4,5},{5,6},{6,7},{8,9},{9,10},{10,11},{11... | collective-permute-start | bytes 41480 | tf_op jit(solution)/shard_map/ppermute | solution.py:17
  43.0 22.2 %collective-permute-start.3 = (f32[3,1,16,128]{3,2,1,0:T(8,128)}, f32[3,1,16,128]{3,2,1,0:T(8,128)}, u32[]{:S(2)}, u32[]{:S(2)}) collective-permute-start(f32[3,1,16,128]{3,2,1,0:T(8,128)} %slice.1183), channel_id=1, source_target_pairs={{0,8},{8,16},{16,24},{24,32},{32,40},{40,48},{48,56},{56,64},{64,7... | collective-permute-start | bytes 73736 | tf_op jit(solution)/shard_map/ppermute | solution.py:17
  209.8 4.6 %collective-permute-start.4 = (f32[3,1,16,128]{3,2,1,0:T(8,128)S(1)}, f32[3,1,16,128]{3,2,1,0:T(8,128)S(1)}, u32[]{:S(2)}, u32[]{:S(2)}) collective-permute-start(f32[3,1,16,128]{3,2,1,0:T(8,128)S(1)} %slice.1185), channel_id=1, source_target_pairs={{8,0},{16,8},{24,16},{32,24},{40,32},{48,40},{56,48},{64,56},{72,6... | collective-permute-start | bytes 73736 | tf_op jit(solution)/shard_map/ppermute | solution.py:17
  214.4 6.5 %collective-permute-start.5 = (f32[3,9,1,128]{3,2,1,0:T(1,128)S(1)}, f32[3,9,1,128]{3,2,1,0:T(1,128)S(1)}, u32[]{:S(2)}, u32[]{:S(2)}) collective-permute-start(f32[3,9,1,128]{3,2,1,0:T(1,128)S(1)} %pad_maximum_fusion.23), channel_id=1, source_target_pairs={{1,0},{2,1},{3,2},{4,3},{5,4},{6,5},{7,6},{9,8},{10,9},{11,10},{12... | collective-permute-start | bytes 41480 | tf_op jit(solution)/shard_map/ppermute | solution.py:17
  226.7 3.1 collective-permute-start.6
  229.9 6.7 %collective-permute-start.7 = (f32[3,1,16,128]{3,2,1,0:T(8,128)S(1)}, f32[3,1,16,128]{3,2,1,0:T(8,128)S(1)}, u32[]{:S(2)}, u32[]{:S(2)}) collective-permute-start(f32[3,1,16,128]{3,2,1,0:T(8,128)S(1)} %slice.1204), channel_id=1, source_target_pairs={{0,8},{8,16},{16,24},{24,32},{32,40},{40,48},{48,56},{56,64},{64,7... | collective-permute-start | bytes 73736 | tf_op jit(solution)/shard_map/ppermute | solution.py:17
  231.9 17.7 %copy-start.14 = (f32[1,8,16,128]{3,0,2,1:T(1,128)S(1)}, f32[1,8,16,128]{3,0,2,1:T(1,128)}, u32[]{:S(2)}) copy-start(f32[1,8,16,128]{3,0,2,1:T(1,128)} %copy-done.12) | copy-start | bytes 196612
  231.9 17.7 %copy-start.16 = (f32[1,8,16,128]{3,0,2,1:T(1,128)S(1)}, f32[1,8,16,128]{3,0,2,1:T(1,128)}, u32[]{:S(2)}) copy-start(f32[1,8,16,128]{3,0,2,1:T(1,128)} %copy-done.15) | copy-start | bytes 196612
  232.0 17.7 %copy-start.18 = (f32[1,8,16,128]{3,0,2,1:T(1,128)S(1)}, f32[1,8,16,128]{3,0,2,1:T(1,128)}, u32[]{:S(2)}) copy-start(f32[1,8,16,128]{3,0,2,1:T(1,128)} %copy-done.17) | copy-start | bytes 196612
  232.0 17.7 %copy-start.20 = (f32[1,8,16,128]{3,0,2,1:T(1,128)S(1)}, f32[1,8,16,128]{3,0,2,1:T(1,128)}, u32[]{:S(2)}) copy-start(f32[1,8,16,128]{3,0,2,1:T(1,128)} %copy-done.19) | copy-start | bytes 196612
  232.0 17.7 %copy-start.22 = (f32[1,8,16,128]{3,0,2,1:T(1,128)S(1)}, f32[1,8,16,128]{3,0,2,1:T(1,128)}, u32[]{:S(2)}) copy-start(f32[1,8,16,128]{3,0,2,1:T(1,128)} %copy-done.21) | copy-start | bytes 196612
  232.0 17.7 %copy-start.28 = (f32[1,8,16,128]{3,2,1,0:T(8,128)S(1)}, f32[1,8,16,128]{3,2,1,0:T(8,128)}, u32[]{:S(2)}) copy-start(f32[1,8,16,128]{3,2,1,0:T(8,128)} %copy-done.27) | copy-start | bytes 196612
  232.0 17.7 %copy-start.30 = (f32[1,8,16,128]{3,2,1,0:T(8,128)S(1)}, f32[1,8,16,128]{3,2,1,0:T(8,128)}, u32[]{:S(2)}) copy-start(f32[1,8,16,128]{3,2,1,0:T(8,128)} %copy-done.29) | copy-start | bytes 196612
  232.0 17.7 %copy-start.32 = (f32[1,8,16,128]{3,2,1,0:T(8,128)S(1)}, f32[1,8,16,128]{3,2,1,0:T(8,128)}, u32[]{:S(2)}) copy-start(f32[1,8,16,128]{3,2,1,0:T(8,128)} %copy-done.31) | copy-start | bytes 196612
  232.0 17.7 %copy-start.34 = (f32[1,8,16,128]{3,2,1,0:T(8,128)S(1)}, f32[1,8,16,128]{3,2,1,0:T(8,128)}, u32[]{:S(2)}) copy-start(f32[1,8,16,128]{3,2,1,0:T(8,128)} %copy-done.33) | copy-start | bytes 196612
  232.0 17.7 %copy-start.36 = (f32[1,8,16,128]{3,2,1,0:T(8,128)S(1)}, f32[1,8,16,128]{3,2,1,0:T(8,128)}, u32[]{:S(2)}) copy-start(f32[1,8,16,128]{3,2,1,0:T(8,128)} %copy-done.35) | copy-start | bytes 196612
  232.0 17.7 %copy-start.127 = (f32[1,8,16,128]{3,2,1,0:T(8,128)S(1)}, f32[1,8,16,128]{3,2,1,0:T(8,128)}, u32[]{:S(2)}) copy-start(f32[1,8,16,128]{3,2,1,0:T(8,128)} %copy-done.126) | copy-start | bytes 196612
  232.0 17.7 %copy-start.129 = (f32[1,8,16,128]{3,2,1,0:T(8,128)S(1)}, f32[1,8,16,128]{3,2,1,0:T(8,128)}, u32[]{:S(2)}) copy-start(f32[1,8,16,128]{3,2,1,0:T(8,128)} %copy-done.128) | copy-start | bytes 196612
  232.1 17.7 %copy-start.131 = (f32[1,8,16,128]{3,2,1,0:T(8,128)S(1)}, f32[1,8,16,128]{3,2,1,0:T(8,128)}, u32[]{:S(2)}) copy-start(f32[1,8,16,128]{3,2,1,0:T(8,128)} %copy-done.130) | copy-start | bytes 196612
  232.1 17.7 %copy-start.133 = (f32[1,8,16,128]{3,2,1,0:T(8,128)S(1)}, f32[1,8,16,128]{3,2,1,0:T(8,128)}, u32[]{:S(2)}) copy-start(f32[1,8,16,128]{3,2,1,0:T(8,128)} %copy-done.132) | copy-start | bytes 196612
  232.1 17.7 %copy-start.135 = (f32[1,8,16,128]{3,2,1,0:T(8,128)S(1)}, f32[1,8,16,128]{3,2,1,0:T(8,128)}, u32[]{:S(2)}) copy-start(f32[1,8,16,128]{3,2,1,0:T(8,128)} %copy-done.134) | copy-start | bytes 196612
  232.1 17.7 %copy-start.137 = (f32[1,8,16,128]{3,2,1,0:T(8,128)S(1)}, f32[1,8,16,128]{3,2,1,0:T(8,128)}, u32[]{:S(2)}) copy-start(f32[1,8,16,128]{3,2,1,0:T(8,128)} %copy-done.136) | copy-start | bytes 196612
  232.1 17.7 %copy-start.139 = (f32[1,8,16,128]{3,2,1,0:T(8,128)S(1)}, f32[1,8,16,128]{3,2,1,0:T(8,128)}, u32[]{:S(2)}) copy-start(f32[1,8,16,128]{3,2,1,0:T(8,128)} %copy-done.138) | copy-start | bytes 196612
  232.1 17.7 %copy-start.141 = (f32[1,8,16,128]{3,2,1,0:T(8,128)S(1)}, f32[1,8,16,128]{3,2,1,0:T(8,128)}, u32[]{:S(2)}) copy-start(f32[1,8,16,128]{3,2,1,0:T(8,128)} %copy-done.140) | copy-start | bytes 196612
  232.1 17.7 %copy-start.143 = (f32[1,8,16,128]{3,2,1,0:T(8,128)S(1)}, f32[1,8,16,128]{3,2,1,0:T(8,128)}, u32[]{:S(2)}) copy-start(f32[1,8,16,128]{3,2,1,0:T(8,128)} %copy-done.142) | copy-start | bytes 196612
  232.1 17.7 %copy-start.145 = (f32[1,8,16,128]{3,2,1,0:T(8,128)S(1)}, f32[1,8,16,128]{3,2,1,0:T(8,128)}, u32[]{:S(2)}) copy-start(f32[1,8,16,128]{3,2,1,0:T(8,128)} %copy-done.144) | copy-start | bytes 196612
  232.1 17.7 %copy-start.147 = (f32[1,8,16,128]{3,2,1,0:T(8,128)S(1)}, f32[1,8,16,128]{3,2,1,0:T(8,128)}, u32[]{:S(2)}) copy-start(f32[1,8,16,128]{3,2,1,0:T(8,128)} %copy-done.146) | copy-start | bytes 196612
  232.1 17.7 %copy-start.149 = (f32[1,8,16,128]{3,2,1,0:T(8,128)S(1)}, f32[1,8,16,128]{3,2,1,0:T(8,128)}, u32[]{:S(2)}) copy-start(f32[1,8,16,128]{3,2,1,0:T(8,128)} %copy-done.148) | copy-start | bytes 196612
  232.2 17.7 %copy-start.151 = (f32[1,8,16,128]{3,2,1,0:T(8,128)S(1)}, f32[1,8,16,128]{3,2,1,0:T(8,128)}, u32[]{:S(2)}) copy-start(f32[1,8,16,128]{3,2,1,0:T(8,128)} %copy-done.150) | copy-start | bytes 196612
  232.2 17.7 %copy-start.153 = (f32[1,8,16,128]{3,2,1,0:T(8,128)S(1)}, f32[1,8,16,128]{3,2,1,0:T(8,128)}, u32[]{:S(2)}) copy-start(f32[1,8,16,128]{3,2,1,0:T(8,128)} %copy-done.152) | copy-start | bytes 196612
  232.2 17.7 %copy-start.155 = (f32[1,8,16,128]{3,2,1,0:T(8,128)S(1)}, f32[1,8,16,128]{3,2,1,0:T(8,128)}, u32[]{:S(2)}) copy-start(f32[1,8,16,128]{3,2,1,0:T(8,128)} %copy-done.154) | copy-start | bytes 196612
  232.2 17.7 %copy-start.157 = (f32[1,8,16,128]{3,2,1,0:T(8,128)S(1)}, f32[1,8,16,128]{3,2,1,0:T(8,128)}, u32[]{:S(2)}) copy-start(f32[1,8,16,128]{3,2,1,0:T(8,128)} %copy-done.156) | copy-start | bytes 196612
  236.7 4.7 %collective-permute-start.8 = (f32[3,1,16,128]{3,2,1,0:T(8,128)S(1)}, f32[3,1,16,128]{3,2,1,0:T(8,128)S(1)}, u32[]{:S(2)}, u32[]{:S(2)}) collective-permute-start(f32[3,1,16,128]{3,2,1,0:T(8,128)S(1)} %slice.1206), channel_id=1, source_target_pairs={{8,0},{16,8},{24,16},{32,24},{40,32},{48,40},{56,48},{64,56},{72,6... | collective-permute-start | bytes 73736 | tf_op jit(solution)/shard_map/ppermute | solution.py:17
  241.4 7.6 %collective-permute-start.9 = (f32[3,9,1,128]{3,2,1,0:T(1,128)S(1)}, f32[3,9,1,128]{3,2,1,0:T(1,128)S(1)}, u32[]{:S(2)}, u32[]{:S(2)}) collective-permute-start(f32[3,9,1,128]{3,2,1,0:T(1,128)S(1)} %pad_maximum_fusion.22), channel_id=1, source_target_pairs={{1,0},{2,1},{3,2},{4,3},{5,4},{6,5},{7,6},{9,8},{10,9},{11,10},{12... | collective-permute-start | bytes 41480 | tf_op jit(solution)/shard_map/ppermute | solution.py:17
  254.7 3.1 collective-permute-start.10
  257.9 6.7 %collective-permute-start.11 = (f32[3,1,16,128]{3,2,1,0:T(8,128)S(1)}, f32[3,1,16,128]{3,2,1,0:T(8,128)S(1)}, u32[]{:S(2)}, u32[]{:S(2)}) collective-permute-start(f32[3,1,16,128]{3,2,1,0:T(8,128)S(1)} %slice.1225), channel_id=1, source_target_pairs={{0,8},{8,16},{16,24},{24,32},{32,40},{40,48},{48,56},{56,64},{64,7... | collective-permute-start | bytes 73736 | tf_op jit(solution)/shard_map/ppermute | solution.py:17
  264.7 4.6 %collective-permute-start.12 = (f32[3,1,16,128]{3,2,1,0:T(8,128)S(1)}, f32[3,1,16,128]{3,2,1,0:T(8,128)S(1)}, u32[]{:S(2)}, u32[]{:S(2)}) collective-permute-start(f32[3,1,16,128]{3,2,1,0:T(8,128)S(1)} %slice.1227), channel_id=1, source_target_pairs={{8,0},{16,8},{24,16},{32,24},{40,32},{48,40},{56,48},{64,56},{72,6... | collective-permute-start | bytes 73736 | tf_op jit(solution)/shard_map/ppermute | solution.py:17
  269.3 7.6 %collective-permute-start.13 = (f32[3,9,1,128]{3,2,1,0:T(1,128)S(1)}, f32[3,9,1,128]{3,2,1,0:T(1,128)S(1)}, u32[]{:S(2)}, u32[]{:S(2)}) collective-permute-start(f32[3,9,1,128]{3,2,1,0:T(1,128)S(1)} %pad_maximum_fusion.21), channel_id=1, source_target_pairs={{1,0},{2,1},{3,2},{4,3},{5,4},{6,5},{7,6},{9,8},{10,9},{11,10},{12... | collective-permute-start | bytes 41480 | tf_op jit(solution)/shard_map/ppermute | solution.py:17
  281.7 3.1 collective-permute-start.14
  284.9 6.7 %collective-permute-start.15 = (f32[3,1,16,128]{3,2,1,0:T(8,128)S(1)}, f32[3,1,16,128]{3,2,1,0:T(8,128)S(1)}, u32[]{:S(2)}, u32[]{:S(2)}) collective-permute-start(f32[3,1,16,128]{3,2,1,0:T(8,128)S(1)} %slice.1246), channel_id=1, source_target_pairs={{0,8},{8,16},{16,24},{24,32},{32,40},{40,48},{48,56},{56,64},{64,7... | collective-permute-start | bytes 73736 | tf_op jit(solution)/shard_map/ppermute | solution.py:17
  291.6 4.6 %collective-permute-start.16 = (f32[3,1,16,128]{3,2,1,0:T(8,128)S(1)}, f32[3,1,16,128]{3,2,1,0:T(8,128)S(1)}, u32[]{:S(2)}, u32[]{:S(2)}) collective-permute-start(f32[3,1,16,128]{3,2,1,0:T(8,128)S(1)} %slice.1248), channel_id=1, source_target_pairs={{8,0},{16,8},{24,16},{32,24},{40,32},{48,40},{56,48},{64,56},{72,6... | collective-permute-start | bytes 73736 | tf_op jit(solution)/shard_map/ppermute | solution.py:17
  296.2 7.6 %collective-permute-start.17 = (f32[3,9,1,128]{3,2,1,0:T(1,128)S(1)}, f32[3,9,1,128]{3,2,1,0:T(1,128)S(1)}, u32[]{:S(2)}, u32[]{:S(2)}) collective-permute-start(f32[3,9,1,128]{3,2,1,0:T(1,128)S(1)} %pad_maximum_fusion.20), channel_id=1, source_target_pairs={{1,0},{2,1},{3,2},{4,3},{5,4},{6,5},{7,6},{9,8},{10,9},{11,10},{12... | collective-permute-start | bytes 41480 | tf_op jit(solution)/shard_map/ppermute | solution.py:17
  309.7 3.1 collective-permute-start.18
  312.9 6.7 %collective-permute-start.19 = (f32[3,1,16,128]{3,2,1,0:T(8,128)S(1)}, f32[3,1,16,128]{3,2,1,0:T(8,128)S(1)}, u32[]{:S(2)}, u32[]{:S(2)}) collective-permute-start(f32[3,1,16,128]{3,2,1,0:T(8,128)S(1)} %slice.1267), channel_id=1, source_target_pairs={{0,8},{8,16},{16,24},{24,32},{32,40},{40,48},{48,56},{56,64},{64,7... | collective-permute-start | bytes 73736 | tf_op jit(solution)/shard_map/ppermute | solution.py:17
  (190 other events, 1235.9 us)
where the time goes:
time: 324 us; the launch traced here: 320 us
  starting transfers between devices  75.9 us (23%)
  matrix products  74.4 us (23%)
  other arithmetic  71.4 us (22%)
  waiting for transfers between devices  56.2 us (17%)
  local copies, waits for them, and re-layouts  37.6 us (12%)
  between operations  4.55 us (1%)
    dot_general x6, matrix products, add_block(): lax.dot_general(column_hot, spread, (((0,), (0,)), ((), ())), precision=l...  72.9 us
    ppermute x20, starting transfers between devices, from_behind(): return lax.ppermute(block, axis, route)  56.9 us
    ppermute x20, waiting for transfers between devices, from_behind(): return lax.ppermute(block, axis, route)  56.2 us
    mul x6, other arithmetic, add_block(): values[:, :, None] * depth_hot[:, None, :]  44.8 us
    dynamic_slice x18, local copies, waits for them, and re-layouts, place_forces(): total, unused = lax.scan(add_block, start, (value_blocks, index_blocks))  13.4 us
    all_to_all x1, starting transfers between devices, per_device(): lax.all_to_all(drm_coef, 'gx', split_axis=0, concat_axis=0, tiled=True)  11.1 us
    unnamed x435, local copies, waits for them, and re-layouts  9.03 us
    add x5, other arithmetic, element_forces(): stress_xx = deviator_sum[0] + pressure  8.58 us
  transfers between devices with their start and end apart: 22, of which 19 were waited for; matrix products, arithmetic and copies ran while one was open for 6% of the time, Pallas kernels for 0%

commit v1 on v0

v1 whole, which is shorter than its diff:
```python
import functools

import jax
import jax.numpy as jnp
from jax import lax
from jax.experimental import pallas as pl
from jax.experimental.pallas import tpu as pltpu
from jax.sharding import PartitionSpec as P

STEPS = 5
SURF = 5
TIME_STEP = 0.7
EX = 8
EY = 16
NZ = 128
PIECE = 384
MESH = pl.DeviceIdType.MESH
F32 = jnp.float32
BF16 = jnp.bfloat16


def lane_next(v):
    lane = lax.broadcasted_iota(jnp.int32, v.shape, 1)
    return jnp.where(lane < NZ - 1, pltpu.roll(v, NZ - 1, 1), 0.0)


def lane_before(v):
    lane = lax.broadcasted_iota(jnp.int32, v.shape, 1)
    return jnp.where(lane > 0, pltpu.roll(v, 1, 1), 0.0)


def strains(near, far):
    ss, ds, sd = [], [], []
    for c in range(3):
        s0, s1 = near[c][0] + near[c][1], far[c][0] + far[c][1]
        d0, d1 = near[c][1] - near[c][0], far[c][1] - far[c][0]
        ss.append(s0 + s1)
        ds.append(s1 - s0)
        sd.append(d0 + d1)

    def both(v):
        return v + lane_next(v)

    xx = 0.25 * both(ds[0])
    yy = 0.25 * both(sd[1])
    zz = 0.25 * (lane_next(ss[2]) - ss[2])
    xy = 0.125 * both(sd[0] + ds[1])
    yz = 0.125 * (lane_next(ss[1] + sd[2]) + (sd[2] - ss[1]))
    zx = 0.125 * (lane_next(ss[0] + ds[2]) + (ds[2] - ss[0]))
    trace = xx + yy + zz
    mean = trace * (1.0 / 3.0)
    return trace, [xx - mean, yy - mean, zz - mean, xy, yz, zx]


def stresses(trace, dev, read_plastic, write_plastic, read_prop):
    total = [None] * 6
    for s in range(SURF):
        shear2 = read_prop(1 + s)
        ratio = read_prop(1 + SURF + s)
        diff = [dev[k] - read_plastic(6 * s + k) for k in range(6)]
        w = diff[0] * diff[0] + diff[1] * diff[1] + diff[2] * diff[2]
        w = w + 2.0 * (diff[3] * diff[3] + diff[4] * diff[4] + diff[5] * diff[5])
        factor = ratio * lax.rsqrt(jnp.maximum(w, ratio * ratio))
        for k in range(6):
            kept = factor * diff[k]
            write_plastic(6 * s + k, dev[k] - kept)
            part = shear2 * kept
            total[k] = part if total[k] is None else total[k] + part
    pressure = read_prop(0) * trace
    return [total[k] + pressure if k < 3 else total[k] for k in range(6)]


def properties(mat, moduli, radii):
    def pick(table, column):
        value = jnp.full(mat.shape, table[0, column], F32)
        for m in range(1, 8):
            value = jnp.where(mat == float(m), table[m, column], value)
        return value

    shear2 = [2.0 * pick(moduli, 1 + s) for s in range(SURF)]
    ratio = [pick(radii, s) / shear2[s] for s in range(SURF)]
    return [pick(moduli, 0)] + shear2 + ratio


def kernel(
    nx, ny,
    disp, velo, plas, mass, mate, moduli, radii, hist, coef, nodes,
    out_disp, out_plas,
    U, V, W, YH, T, CS, CR, PL, PYS, PY, PCS, PCR, PR, PRY, SIG,
    FS, FR, H, B, A, ACC, WM, hv, cv, nv, velv, massv, matev,
    lsem, osem, a_send, a_recv, h_send, h_recv, p_send, p_recv,
):
    gx = lax.axis_index("gx")
    gy = lax.axis_index("gy")
    xn, xp = lax.rem(gx + 1, nx), lax.rem(gx + nx - 1, nx)
    yn, yp = lax.rem(gy + 1, ny), lax.rem(gy + ny - 1, ny)

    barrier = pltpu.get_barrier_semaphore()

    def greet(k, carry):
        pl.semaphore_signal(
            barrier, inc=1, device_id=(lax.rem(gx + k, nx), gy), device_id_type=MESH
        )
        return carry

    lax.fori_loop(1, nx, greet, 0)
    for place in ((gx, yn), (gx, yp), (xn, yn), (xn, yp), (xp, yn), (xp, yp)):
        pl.semaphore_signal(barrier, inc=1, device_id=place, device_id_type=MESH)

    loads = [
        pltpu.make_async_copy(src, dst, lsem.at[i])
        for i, (src, dst) in enumerate(
            (
                (hist, hv),
                (coef, cv),
                (plas, PL.at[pl.ds(0, 6 * SURF), pl.ds(1, EX)]),
                (disp, U.at[1, :, pl.ds(1, EX), pl.ds(0, EY)]),
                (mate, matev),
                (nodes, nv),
                (velo, velv),
                (mass, massv),
            )
        )
    ]
    for load in loads:
        load.start()

    loads[0].wait()
    loads[1].wait()

    def make_forces(a, carry):
        h = [hv[a, pl.ds(l, 19), :] for l in range(3)]
        force = cv[a, 0:1, :] * (h[2] - 2.0 * h[1] + h[0]) + cv[a, 1:2, :] * h[1]
        for n in range(STEPS):
            for c in range(3):
                FS[n, a, :, c * PIECE : (c + 1) * PIECE] = force[c * 7 + n : c * 7 + n + 1, :]
        return carry

    lax.fori_loop(0, nx, make_forces, 0)

    def own_forces(n, carry):
        FR[n, gx] = FS[n, gx]
        return carry

    lax.fori_loop(0, STEPS, own_forces, 0)

    loads[3].wait()

    def pack_rows(x, carry):
        for c in range(3):
            V[0, c, pl.ds(8 + x, 1), :] = U[1, c, x + 1, 0:1, :]
            YH[0, c, pl.ds(x, 1), :] = U[1, c, x + 1, EY - 1 : EY, :]
        return carry

    lax.fori_loop(0, EX, pack_rows, 0)

    def pack_corners(n):
        CS[n, 0] = V[n, :, 8:9, :]
        CS[n, 1] = YH[n, :, 0:1, :]
        CS[n, 2] = V[n, :, 15:16, :]
        CS[n, 3] = YH[n, :, 7:8, :]

    pack_corners(0)

    loads[4].wait()
    PL[6 * SURF, 1 : EX + 1] = matev[...].astype(F32)
    loads[2].wait()

    def pack_plastic(k, carry):
        for x in range(EX):
            PYS[k, x : x + 1, :] = PL[k, x + 1, EY - 1 : EY, :]
        PCS[k] = PYS[k, EX - 1 : EX, :]
        return carry

    lax.fori_loop(0, 6 * SURF + 1, pack_plastic, 0)

    pl.semaphore_wait(barrier, nx - 1 + 6)

    def remote(src, dst, send, recv, place):
        return pltpu.make_async_remote_copy(
            src_ref=src, dst_ref=dst, send_sem=send, recv_sem=recv, device_id=place,
            device_id_type=MESH,
        )

    def send_forces(n):
        def one(k, carry):
            to = lax.rem(gx + k, nx)
            remote(FS.at[n, to], FR.at[n, gx], a_send.at[n], a_recv.at[n], (to, gy)).start()
            return carry

        lax.fori_loop(1, nx, one, 0)

    def forces_done(n):
        some = FR.at[n, pl.ds(0, nx - 1)]
        return (
            pltpu.make_async_copy(some, some, a_send.at[n]),
            pltpu.make_async_copy(some, some, a_recv.at[n]),
        )

    def halo(n):
        own = pl.ds(0, EY)
        pairs = (
            (U.at[n + 1, :, 1, own], U.at[n + 1, :, EX + 1, own], (xp, gy)),
            (U.at[n + 1, :, EX, own], U.at[n + 1, :, 0, own], (xn, gy)),
            (V.at[n, :, pl.ds(8, 8)], T.at[n], (gx, yp)),
            (YH.at[n], W.at[n, :, pl.ds(8, 8)], (gx, yn)),
            (CS.at[n, 0], CR.at[n, 0], (xp, yp)),
            (CS.at[n, 1], CR.at[n, 1], (xp, yn)),
            (CS.at[n, 2], CR.at[n, 2], (xn, yp)),
            (CS.at[n, 3], CR.at[n, 3], (xn, yn)),
        )
        return [
            remote(src, dst, h_send.at[n, i], h_recv.at[n, i], place)
            for i, (src, dst, place) in enumerate(pairs)
        ]

    def plastic_halo():
        pairs = (
            (PL.at[:, EX], PL.at[:, 0], (xn, gy)),
            (PYS, PY.at[:, pl.ds(8, 8)], (gx, yn)),
            (PCS, PCR, (xn, yn)),
        )
        return [
            remote(src, dst, p_send.at[i], p_recv.at[i], place)
            for i, (src, dst, place) in enumerate(pairs)
        ]

    for copy in halo(0):
        copy.start()
    send_forces(0)
    for copy in plastic_halo():
        copy.start()
    send_forces(1)

    loads[5].wait()

    def one_hot(r, carry):
        v = nv[:, pl.ds(pl.multiple_of(r * PIECE, 128), PIECE)]
        high = (v // 2048) * 8 + (v // 128) % 8
        low = ((v // 1024) % 2) * 128 + v % 128
        rows = lax.broadcasted_iota(jnp.int32, (64, PIECE), 0)
        H[r] = jnp.where(rows == high, 1.0, 0.0).astype(BF16)
        rows = lax.broadcasted_iota(jnp.int32, (256, PIECE), 0)
        B[r] = jnp.where(rows == low, 1.0, 0.0).astype(BF16)
        return carry

    lax.fori_loop(0, nx, one_hot, 0)

    def own_props(x, carry):
        for k, value in enumerate(properties(PL[6 * SURF, x], moduli, radii)):
            PR[k, x] = value
        return carry

    lax.fori_loop(1, EX + 1, own_props, 0)

    for load in loads[6:]:
        load.wait()
    WM[...] = (TIME_STEP * TIME_STEP) / massv[...]
    U[0, :, 1 : EX + 1, 0:EY] = U[1, :, 1 : EX + 1, 0:EY] - TIME_STEP * velv[...]

    for copy in plastic_halo():
        copy.wait()
    PY[:, 7:8, :] = PCR[...]
    live_x = jnp.where(gx > 0, 1.0, 0.0).astype(F32)
    live_y = jnp.where(gy > 0, 1.0, 0.0).astype(F32)
    for k, value in enumerate(properties(PL[6 * SURF, 0], moduli, radii)):
        PR[k, 0] = value * live_x if k <= SURF else value
    row = lax.broadcasted_iota(jnp.int32, (16, NZ), 0)
    live = jnp.where(row <= 7, live_x * live_y, live_y)
    for k, value in enumerate(properties(PY[6 * SURF], moduli, radii)):
        PRY[k] = value * live if k <= SURF else value

    def scatter(n):
        ACC[...] = jnp.zeros_like(ACC)

        def pair(j, carry):
            for p in (0, 1):
                r = 2 * j + p
                v = jnp.broadcast_to(FR[n, r], (16, 3 * PIECE))
                head = v.astype(BF16)
                tail = (v - head.astype(F32)).astype(BF16)
                for g in range(4):
                    hot = H[r, g * 16 : (g + 1) * 16, :]
                    for i, part in enumerate((head, tail)):
                        for c in range(3):
                            top = (i * 3 + c) * 64 + g * 16
                            A[top : top + 16, p * PIECE : (p + 1) * PIECE] = (
                                hot * part[:, c * PIECE : (c + 1) * PIECE]
                            )
            both = jnp.concatenate([B[2 * j], B[2 * j + 1]], axis=1)
            ACC[...] += lax.dot_general(
                A[...], both, (((1,), (1,)), ((), ())), preferred_element_type=F32
            )
            return carry

        lax.fori_loop(0, nx // 2, pair, 0)

    def step(n, carry):
        for copy in forces_done(n):
            copy.wait()
        scatter(n)

        copies = halo(n)
        for copy in copies:
            copy.wait_recv()

        def unpack(x, inner):
            for c in range(3):
                U[n + 1, c, x + 1, EY : EY + 1, :] = T[n, c, pl.ds(x, 1), :]
            return inner

        lax.fori_loop(0, EX, unpack, 0)
        U[n + 1, :, EX + 1, EY : EY + 1, :] = CR[n, 0]
        W[n, :, 16:17, :] = CR[n, 1]
        U[n + 1, :, 0, EY : EY + 1, :] = CR[n, 2]
        W[n, :, 7:8, :] = CR[n, 3]

        @pl.when(gx == nx - 1)
        def _():
            U[n + 1, :, EX + 1] = jnp.zeros((3, 24, NZ), F32)
            W[n, :, 16:17, :] = jnp.zeros((3, 1, NZ), F32)

        @pl.when(gy == ny - 1)
        def _():
            U[n + 1, :, :, EY : EY + 8] = jnp.zeros((3, EX + 2, 8, NZ), F32)

        V[n, :, 7:8, :] = U[n + 1, :, 0, 0:1, :]
        V[n, :, 16:17, :] = U[n + 1, :, EX + 1, 0:1, :]

        for t in range(2):
            lo = pl.ds(t * 8, 8)
            up = pl.ds(t * 8 + 1, 8)
            near = [(W[n, c, lo, :], V[n, c, lo, :]) for c in range(3)]
            far = [(W[n, c, up, :], V[n, c, up, :]) for c in range(3)]
            trace, dev = strains(near, far)

            def write(k, value):
                PY[k, lo, :] = value

            sigma = stresses(trace, dev, lambda k: PY[k, lo, :], write, lambda k: PRY[k, lo, :])
            for k in range(6):
                if t == 0:
                    SIG[k, 0, 7:8, :] = sigma[k][7:8, :]
                else:
                    for x in range(EX):
                        SIG[k, x + 1, 7:8, :] = sigma[k][x : x + 1, :]

        def elements(x, inner):
            for t in range(2):
                lo = pl.ds(t * 8, 8)
                up = pl.ds(t * 8 + 1, 8)
                near = [(U[n + 1, c, x, lo, :], U[n + 1, c, x, up, :]) for c in range(3)]
                far = [(U[n + 1, c, x + 1, lo, :], U[n + 1, c, x + 1, up, :]) for c in range(3)]
                trace, dev = strains(near, far)

                def write(k, value):
                    PL[k, x, lo, :] = value

                sigma = stresses(
                    trace, dev, lambda k: PL[k, x, lo, :], write, lambda k: PR[k, x, lo, :]
                )
                for k in range(6):
                    SIG[k, x, t * 8 + 8 : t * 8 + 16, :] = sigma[k]
            return inner

        lax.fori_loop(0, EX + 1, elements, 0)

        def update(x, inner):
            for t in range(2):
                old = pl.ds(t * 8 + 7, 8)
                new = pl.ds(t * 8 + 8, 8)
                lo = pl.ds(t * 8, 8)
                minus, plus = {}, {}
                for k in range(6):
                    for rows in (0, 1):
                        at = new if rows else old
                        before, here = SIG[k, x, at, :], SIG[k, x + 1, at, :]
                        plus[k, rows] = before + here
                        if k in (0, 3, 5):
                            minus[k, rows] = before - here
                for c, (kx, ky, kz) in enumerate(((0, 3, 5), (3, 1, 4), (5, 4, 2))):
                    across = (minus[kx, 0] + plus[ky, 0]) + (minus[kx, 1] - plus[ky, 1])
                    down = plus[kz, 0] + plus[kz, 1]
                    inside = lane_before(across + down) + (across - down)
                    top = c * 64 + x * 8
                    lanes = slice(t * 128, (t + 1) * 128)
                    placed = ACC[pl.ds(top, 8), lanes] + ACC[pl.ds(192 + top, 8), lanes]
                    now = U[n + 1, c, x + 1, lo, :]
                    later = (
                        2.0 * now
                        - U[n, c, x + 1, lo, :]
                        + WM[x, lo, :] * (placed - 0.25 * inside)
                    )
                    U[n + 2, c, x + 1, lo, :] = later
                    if t == 0:
                        V[n + 1, c, pl.ds(8 + x, 1), :] = later[0:1, :]
                    else:
                        YH[n + 1, c, pl.ds(x, 1), :] = later[7:8, :]
            return inner

        lax.fori_loop(0, EX, update, 0)

        @pl.when(n < STEPS - 1)
        def _():
            pack_corners(n + 1)
            for copy in halo(n + 1):
                copy.start()

        @pl.when(n < STEPS - 2)
        def _():
            send_forces(n + 2)

        for copy in copies:
            copy.wait_send()
        return carry

    lax.fori_loop(0, STEPS, step, 0)
    outs = [
        pltpu.make_async_copy(
            U.at[STEPS + 1, :, pl.ds(1, EX), pl.ds(0, EY)], out_disp, osem.at[0]
        ),
        pltpu.make_async_copy(PL.at[pl.ds(0, 6 * SURF), pl.ds(1, EX)], out_plas, osem.at[1]),
    ]
    for out in outs:
        out.start()
    for out in outs:
        out.wait()


def per_device(nx, ny, *args):
    any_space = pl.BlockSpec(memory_space=pl.ANY)
    smem = pl.BlockSpec(memory_space=pltpu.SMEM)
    vmem = pltpu.VMEM
    dma = pltpu.SemaphoreType.DMA
    scratch = [
        vmem((STEPS + 2, 3, EX + 2, EY + 8, NZ), F32),
        vmem((STEPS + 1, 3, 24, NZ), F32),
        vmem((STEPS, 3, 24, NZ), F32),
        vmem((STEPS + 1, 3, 8, NZ), F32),
        vmem((STEPS, 3, 8, NZ), F32),
        vmem((STEPS, 4, 3, 1, NZ), F32),
        vmem((STEPS, 4, 3, 1, NZ), F32),
        vmem((6 * SURF + 1, EX + 1, EY, NZ), F32),
        vmem((6 * SURF + 1, EX, NZ), F32),
        vmem((6 * SURF + 1, 16, NZ), F32),
        vmem((6 * SURF + 1, 1, NZ), F32),
        vmem((6 * SURF + 1, 1, NZ), F32),
        vmem((1 + 2 * SURF, EX + 1, EY, NZ), F32),
        vmem((1 + 2 * SURF, 16, NZ), F32),
        vmem((6, EX + 1, EY + 8, NZ), F32),
        vmem((STEPS, nx, 1, 3 * PIECE), F32),
        vmem((STEPS, nx, 1, 3 * PIECE), F32),
        vmem((nx, 64, PIECE), BF16),
        vmem((nx, 256, PIECE), BF16),
        vmem((384, 2 * PIECE), BF16),
        vmem((384, 256), F32),
        vmem((EX, EY, NZ), F32),
        vmem((nx, 21, PIECE), F32),
        vmem((nx, 2, PIECE), F32),
        vmem((1, nx * PIECE), jnp.int32),
        vmem((3, EX, EY, NZ), F32),
        vmem((EX, EY, NZ), F32),
        vmem((EX, EY, NZ), jnp.int32),
        dma((8,)),
        dma((2,)),
        dma((STEPS,)),
        dma((STEPS,)),
        dma((STEPS, 8)),
        dma((STEPS, 8)),
        dma((3,)),
        dma((3,)),
    ]
    return pl.pallas_call(
        functools.partial(kernel, nx, ny),
        out_shape=(
            jax.ShapeDtypeStruct((3, EX, EY, NZ), F32),
            jax.ShapeDtypeStruct((6 * SURF, EX, EY, NZ), F32),
        ),
        in_specs=[any_space] * 5 + [smem] * 2 + [any_space] * 3,
        out_specs=(any_space, any_space),
        scratch_shapes=scratch,
        compiler_params=pltpu.CompilerParams(
            collective_id=0, has_side_effects=True, vmem_limit_bytes=48 * 1024 * 1024
        ),
        name="box_steps",
    )(*args)


def solution(mesh):
    return jax.shard_map(
        functools.partial(per_device, mesh.shape["gx"], mesh.shape["gy"]),
        mesh=mesh,
        in_specs=(
            P(None, "gx", "gy", None),
            P(None, "gx", "gy", None),
            P(None, "gx", "gy", None),
            P("gx", "gy", None),
            P("gx", "gy", None),
            P(),
            P(),
            P("gx", None, "gy"),
            P("gx", None, "gy"),
            P("gx", "gy"),
        ),
        out_specs=(P(None, "gx", "gy", None), P(None, "gx", "gy", None)),
        check_vma=False,
    )
```

time: 324 us -> 77.5 us (0.24)
  starting transfers between devices: 75.9 us -> 0 us
  matrix products: 74.4 us -> 0 us
  other arithmetic: 71.4 us -> 0 us
  Pallas kernels: 0 us -> 66.8 us
  waiting for transfers between devices: 56.2 us -> 0 us
  local copies, waits for them, and re-layouts: 37.6 us -> 8.81 us
  between operations: 4.55 us -> 0.7 us
    dot_general x7 -> x0, matrix products: 74.4 us -> none  [the longest x6 72.9 us: add_block(): lax.dot_general(column_hot, spread, (((0,), (0,)), ((), ())), precision=l...]
    pallas_call x0 -> x1, Pallas kernels: none -> 66.8 us  [per_device(): pl.pallas_call(functools.partial(kernel, nx, ny), out_shape=(jax.ShapeDty...]
    ppermute x20 -> x0, starting transfers between devices: 56.9 us -> none  [from_behind(): return lax.ppermute(block, axis, route)]
    ppermute x20 -> x0, waiting for transfers between devices: 56.2 us -> none  [from_behind(): return lax.ppermute(block, axis, route)]
    mul x11 -> x0, other arithmetic: 48.1 us -> none  [the longest x6 44.8 us: add_block(): values[:, :, None] * depth_hot[:, None, :]]
    all_to_all x2 -> x0, starting transfers between devices: 19 us -> none  [the longest x1 11.1 us: per_device(): lax.all_to_all(drm_coef, 'gx', split_axis=0, concat_axis=0, tiled=True)]
    add x56 -> x0, other arithmetic: 16.6 us -> none  [the longest x5 8.58 us: element_forces(): stress_xx = deviator_sum[0] + pressure]
    dynamic_slice x18 -> x0, local copies, waits for them, and re-layouts: 13.4 us -> none  [place_forces(): total, unused = lax.scan(add_block, start, (value_blocks, index_blocks))]
  transfers between devices with their start and end apart: 22 -> 0, of which waited for: 19 -> 0; matrix products, arithmetic and copies ran while one was open for 6% -> 0% of each run, Pallas kernels for 0% -> 0%
where the time goes in v1:
time: 77.5 us; the launch traced here: 76.3 us
  Pallas kernels  66.8 us (86%)
  local copies, waits for them, and re-layouts  8.81 us (11%)
    pallas_call x1, Pallas kernels, per_device(): pl.pallas_call(functools.partial(kernel, nx, ny), out_shape=(jax.ShapeDty...  66.8 us
    unnamed x21, local copies, waits for them, and re-layouts  8.81 us

profile of v1, /device:TPU:3, one launch (start us, length us, event | category | flops | bytes accessed | tf_op | source)
XLA Modules:
  0.0 76.3 jit_solution(38100647903973713)
XLA Ops:
  0.6 0.0 copy-start.6
  0.6 0.0 copy-start
  0.7 0.0 copy-start.1
  0.7 2.0 %copy.12.hist = f32[32,21,384]{2,1,0:T(8,128)S(1)} copy(f32[32,21,384]{2,0,1:T(8,128)} %param.17) | data formatting | bytes 2064384 | tf_op args[7]
  2.6 0.0 copy-done.6
  2.7 0.0 copy-done
  2.7 0.0 copy-done.1
  2.7 0.0 copy-start.2
  2.7 0.9 %copy-done.2 = f32[3,8,16,128]{3,2,1,0:T(8,128)S(1)} copy-done((f32[3,8,16,128]{3,2,1,0:T(8,128)S(1)}, f32[3,8,16,128]{3,2,1,0:T(8,128)}, u32[]{:S(2)}) %copy-start.2) | copy-done | bytes 196632
  3.6 0.0 copy-start.3
  3.6 0.9 %copy-done.3 = f32[32,2,384]{2,1,0:T(2,128)S(1)} copy-done((f32[32,2,384]{2,1,0:T(2,128)S(1)}, f32[32,2,384]{2,1,0:T(2,128)}, u32[]{:S(2)}) %copy-start.3) | copy-done | bytes 98328
  4.5 0.0 copy-start.4
  4.5 0.8 %copy-done.4 = f32[8,16,128]{2,1,0:T(8,128)S(1)} copy-done((f32[8,16,128]{2,1,0:T(8,128)S(1)}, f32[8,16,128]{2,1,0:T(8,128)}, u32[]{:S(2)}) %copy-start.4) | copy-done | bytes 65560
  5.3 0.0 copy-start.5
  5.3 0.8 %copy-done.5 = s32[8,16,128]{2,1,0:T(8,128)S(1)} copy-done((s32[8,16,128]{2,1,0:T(8,128)S(1)}, s32[8,16,128]{2,1,0:T(8,128)}, u32[]{:S(2)}) %copy-start.5) | copy-done | bytes 65560
  6.2 0.0 copy-start.7
  6.2 0.7 copy-done.7
  6.9 0.0 copy-start.8
  6.9 0.7 copy-done.8
  7.5 66.8 %box_steps.1 = (f32[3,8,16,128]{3,2,1,0:T(8,128)S(1)}, f32[30,8,16,128]{3,2,1,0:T(8,128)S(1)}) custom-call(f32[3,8,16,128]{3,2,1,0:T(8,128)S(1)} %copy-done.1, f32[3,8,16,128]{3,2,1,0:T(8,128)S(1)} %copy-done.2, f32[30,8,16,128]{3,2,1,0:T(8,128)S(1)} %copy-done, f32[8,16,128]{2,1,0:T(8,128)S(1)} %copy-done.4, s32[8,16,128]{2,1,0:T(8,128)S(1)} %copy-done.5, ...), custom_call_target="tpu_custom_call" | custom-call | tf_op jit(solution)/shard_map/box_steps/pallas_call | solution.py:473
  74.3 0.7 copy.15
  75.0 1.3 %copy.16 = f32[30,8,16,128]{3,2,1,0:T(8,128)} copy(f32[30,8,16,128]{3,2,1,0:T(8,128)S(1)} %get-tuple-element.5) | data formatting | bytes 3932160
Async XLA Ops:
  0.6 2.0 %copy-start.6 = (s32[1,12288]{1,0:T(1,128)S(1)}, s32[1,12288]{1,0:T(1,128)}, u32[]{:S(2)}) copy-start(s32[1,12288]{1,0:T(1,128)} %nodes.1) | copy-start | bytes 147460
  0.6 2.0 %copy-start = (f32[30,8,16,128]{3,2,1,0:T(8,128)S(1)}, f32[30,8,16,128]{3,2,1,0:T(8,128)}, u32[]{:S(2)}) copy-start(f32[30,8,16,128]{3,2,1,0:T(8,128)} %plas.1) | copy-start | bytes 5898244
  0.7 2.0 %copy-start.1 = (f32[3,8,16,128]{3,2,1,0:T(8,128)S(1)}, f32[3,8,16,128]{3,2,1,0:T(8,128)}, u32[]{:S(2)}) copy-start(f32[3,8,16,128]{3,2,1,0:T(8,128)} %disp.1) | copy-start | bytes 589828
  2.7 0.9 %copy-start.2 = (f32[3,8,16,128]{3,2,1,0:T(8,128)S(1)}, f32[3,8,16,128]{3,2,1,0:T(8,128)}, u32[]{:S(2)}) copy-start(f32[3,8,16,128]{3,2,1,0:T(8,128)} %velo.1) | copy-start | bytes 589828
  3.6 0.9 %copy-start.3 = (f32[32,2,384]{2,1,0:T(2,128)S(1)}, f32[32,2,384]{2,1,0:T(2,128)}, u32[]{:S(2)}) copy-start(f32[32,2,384]{2,1,0:T(2,128)} %coef.1) | copy-start | bytes 294916
  4.5 0.8 %copy-start.4 = (f32[8,16,128]{2,1,0:T(8,128)S(1)}, f32[8,16,128]{2,1,0:T(8,128)}, u32[]{:S(2)}) copy-start(f32[8,16,128]{2,1,0:T(8,128)} %mass.1) | copy-start | bytes 196612
  5.3 0.8 %copy-start.5 = (s32[8,16,128]{2,1,0:T(8,128)S(1)}, s32[8,16,128]{2,1,0:T(8,128)}, u32[]{:S(2)}) copy-start(s32[8,16,128]{2,1,0:T(8,128)} %mate.1) | copy-start | bytes 196612
  6.2 0.7 copy-start.7
  6.9 0.7 copy-start.8

commit v2 on v1

--- a/solution.py
+++ b/solution.py
@@ -87,7 +87,7 @@
     disp, velo, plas, mass, mate, moduli, radii, hist, coef, nodes,
     out_disp, out_plas,
     U, V, W, YH, T, CS, CR, PL, PYS, PY, PCS, PCR, PR, PRY, SIG,
-    FS, FR, H, B, A, ACC, WM, hv, cv, nv, velv, massv, matev,
+    FS, FR, H, B, A, ACC, WM, hv, cv, ct, nv, velv, massv, matev,
     lsem, osem, a_send, a_recv, h_send, h_recv, p_send, p_recv,
 ):
     gx = lax.axis_index("gx")
@@ -128,15 +128,25 @@
     loads[0].wait()
     loads[1].wait()
 
-    def make_forces(a, carry):
-        h = [hv[a, pl.ds(l, 19), :] for l in range(3)]
-        force = cv[a, 0:1, :] * (h[2] - 2.0 * h[1] + h[0]) + cv[a, 1:2, :] * h[1]
-        for n in range(STEPS):
-            for c in range(3):
-                FS[n, a, :, c * PIECE : (c + 1) * PIECE] = force[c * 7 + n : c * 7 + n + 1, :]
-        return carry
-
-    lax.fori_loop(0, nx, make_forces, 0)
+    def split_coef(a, carry):
+        for j in range(2):
+            ct[j, pl.ds(a, 1), :] = cv[a, j : j + 1, :]
+        return carry
+
+    lax.fori_loop(0, nx, split_coef, 0, unroll=4)
+
+    def make_forces(g, carry):
+        rows = pl.ds(pl.multiple_of(g * 8, 8), 8)
+        cm, ck = ct[0, rows, :], ct[1, rows, :]
+        for c in range(3):
+            h = [hv[c * 7 + l, rows, :] for l in range(STEPS + 2)]
+            for n in range(STEPS):
+                force = cm * (h[n + 2] - 2.0 * h[n + 1] + h[n]) + ck * h[n + 1]
+                for i in range(8):
+                    FS[n, g * 8 + i, :, c * PIECE : (c + 1) * PIECE] = force[i : i + 1, :]
+        return carry
+
+    lax.fori_loop(0, nx // 8, make_forces, 0)
 
     def own_forces(n, carry):
         FR[n, gx] = FS[n, gx]
@@ -241,7 +251,8 @@
         rows = lax.broadcasted_iota(jnp.int32, (64, PIECE), 0)
         H[r] = jnp.where(rows == high, 1.0, 0.0).astype(BF16)
         rows = lax.broadcasted_iota(jnp.int32, (256, PIECE), 0)
-        B[r] = jnp.where(rows == low, 1.0, 0.0).astype(BF16)
+        at = pl.ds(pl.multiple_of(r * PIECE, 128), PIECE)
+        B[:, at] = jnp.where(rows == low, 1.0, 0.0).astype(BF16)
         return carry
 
     lax.fori_loop(0, nx, one_hot, 0)
@@ -258,47 +269,50 @@
     WM[...] = (TIME_STEP * TIME_STEP) / massv[...]
     U[0, :, 1 : EX + 1, 0:EY] = U[1, :, 1 : EX + 1, 0:EY] - TIME_STEP * velv[...]
 
-    for copy in plastic_halo():
-        copy.wait()
-    PY[:, 7:8, :] = PCR[...]
-    live_x = jnp.where(gx > 0, 1.0, 0.0).astype(F32)
-    live_y = jnp.where(gy > 0, 1.0, 0.0).astype(F32)
-    for k, value in enumerate(properties(PL[6 * SURF, 0], moduli, radii)):
-        PR[k, 0] = value * live_x if k <= SURF else value
-    row = lax.broadcasted_iota(jnp.int32, (16, NZ), 0)
-    live = jnp.where(row <= 7, live_x * live_y, live_y)
-    for k, value in enumerate(properties(PY[6 * SURF], moduli, radii)):
-        PRY[k] = value * live if k <= SURF else value
-
     def scatter(n):
-        ACC[...] = jnp.zeros_like(ACC)
-
-        def pair(j, carry):
-            for p in (0, 1):
-                r = 2 * j + p
-                v = jnp.broadcast_to(FR[n, r], (16, 3 * PIECE))
-                head = v.astype(BF16)
-                tail = (v - head.astype(F32)).astype(BF16)
-                for g in range(4):
-                    hot = H[r, g * 16 : (g + 1) * 16, :]
-                    for i, part in enumerate((head, tail)):
-                        for c in range(3):
-                            top = (i * 3 + c) * 64 + g * 16
-                            A[top : top + 16, p * PIECE : (p + 1) * PIECE] = (
-                                hot * part[:, c * PIECE : (c + 1) * PIECE]
-                            )
-            both = jnp.concatenate([B[2 * j], B[2 * j + 1]], axis=1)
-            ACC[...] += lax.dot_general(
-                A[...], both, (((1,), (1,)), ((), ())), preferred_element_type=F32
-            )
+        def spread(r, carry):
+            v = jnp.broadcast_to(FR[n, r], (16, 3 * PIECE))
+            head = v.astype(BF16)
+            tail = (v - head.astype(F32)).astype(BF16)
+            at = pl.ds(pl.multiple_of(r * PIECE, 128), PIECE)
+            for g in range(4):
+                hot = H[r, g * 16 : (g + 1) * 16, :]
+                for i, part in enumerate((head, tail)):
+                    for c in range(3):
+                        top = (i * 3 + c) * 64 + g * 16
+                        A[top : top + 16, at] = hot * part[:, c * PIECE : (c + 1) * PIECE]
             return carry
 
-        lax.fori_loop(0, nx // 2, pair, 0)
+        lax.fori_loop(0, nx, spread, 0, unroll=nx)
+        ACC[...] = lax.dot_general(
+            A[...], B[...], (((1,), (1,)), ((), ())), preferred_element_type=F32
+        )
+
+    outs = [
+        pltpu.make_async_copy(
+            U.at[STEPS + 1, :, pl.ds(1, EX), pl.ds(0, EY)], out_disp, osem.at[0]
+        ),
+        pltpu.make_async_copy(PL.at[pl.ds(0, 6 * SURF), pl.ds(1, EX)], out_plas, osem.at[1]),
+    ]
 
     def step(n, carry):
         for copy in forces_done(n):
             copy.wait()
         scatter(n)
+
+        @pl.when(n == 0)
+        def _():
+            for copy in plastic_halo():
+                copy.wait()
+            PY[:, 7:8, :] = PCR[...]
+            live_x = jnp.where(gx > 0, 1.0, 0.0).astype(F32)
+            live_y = jnp.where(gy > 0, 1.0, 0.0).astype(F32)
+            for k, value in enumerate(properties(PL[6 * SURF, 0], moduli, radii)):
+                PR[k, 0] = value * live_x if k <= SURF else value
+            row = lax.broadcasted_iota(jnp.int32, (16, NZ), 0)
+            live = jnp.where(row <= 7, live_x * live_y, live_y)
+            for k, value in enumerate(properties(PY[6 * SURF], moduli, radii)):
+                PRY[k] = value * live if k <= SURF else value
 
         copies = halo(n)
         for copy in copies:
@@ -363,7 +377,11 @@
                     SIG[k, x, t * 8 + 8 : t * 8 + 16, :] = sigma[k]
             return inner
 
-        lax.fori_loop(0, EX + 1, elements, 0)
+        lax.fori_loop(0, EX + 1, elements, 0, unroll=EX + 1)
+
+        @pl.when(n == STEPS - 1)
+        def _():
+            outs[1].start()
 
         def update(x, inner):
             for t in range(2):
@@ -398,7 +416,7 @@
                         YH[n + 1, c, pl.ds(x, 1), :] = later[7:8, :]
             return inner
 
-        lax.fori_loop(0, EX, update, 0)
+        lax.fori_loop(0, EX, update, 0, unroll=EX)
 
         @pl.when(n < STEPS - 1)
         def _():
@@ -415,14 +433,7 @@
         return carry
 
     lax.fori_loop(0, STEPS, step, 0)
-    outs = [
-        pltpu.make_async_copy(
-            U.at[STEPS + 1, :, pl.ds(1, EX), pl.ds(0, EY)], out_disp, osem.at[0]
-        ),
-        pltpu.make_async_copy(PL.at[pl.ds(0, 6 * SURF), pl.ds(1, EX)], out_plas, osem.at[1]),
-    ]
-    for out in outs:
-        out.start()
+    outs[0].start()
     for out in outs:
         out.wait()
 
@@ -451,12 +462,13 @@
         vmem((STEPS, nx, 1, 3 * PIECE), F32),
         vmem((STEPS, nx, 1, 3 * PIECE), F32),
         vmem((nx, 64, PIECE), BF16),
-        vmem((nx, 256, PIECE), BF16),
-        vmem((384, 2 * PIECE), BF16),
+        vmem((256, nx * PIECE), BF16),
+        vmem((384, nx * PIECE), BF16),
         vmem((384, 256), F32),
         vmem((EX, EY, NZ), F32),
-        vmem((nx, 21, PIECE), F32),
+        vmem((21, nx, PIECE), F32),
         vmem((nx, 2, PIECE), F32),
+        vmem((2, nx, PIECE), F32),
         vmem((1, nx * PIECE), jnp.int32),
         vmem((3, EX, EY, NZ), F32),
         vmem((EX, EY, NZ), F32),
@@ -480,10 +492,10 @@
         out_specs=(any_space, any_space),
         scratch_shapes=scratch,
         compiler_params=pltpu.CompilerParams(
-            collective_id=0, has_side_effects=True, vmem_limit_bytes=48 * 1024 * 1024
+            collective_id=0, has_side_effects=True, vmem_limit_bytes=60 * 1024 * 1024
         ),
         name="box_steps",
-    )(*args)
+    )(*args[:7], jnp.transpose(args[7], (1, 0, 2)), *args[8:])
 
 
 def solution(mesh):

time: 77.5 us -> 60.7 us (0.78)
  the two profiles are of different devices: /device:TPU:3 before, /device:TPU:1 now
where the time goes in v2:
time: 60.7 us; the launch traced here: 60.5 us
  Pallas kernels  55.3 us (91%)
  local copies, waits for them, and re-layouts  4.63 us (8%)
  between operations  0.64 us (1%)
    pallas_call x1, Pallas kernels, per_device(): pl.pallas_call(functools.partial(kernel, nx, ny), out_shape=(jax.ShapeDty...  55.3 us
    unnamed x2, local copies, waits for them, and re-layouts  4.63 us

profile of v2, /device:TPU:1, one launch (start us, length us, event | category | flops | bytes accessed | tf_op | source)
XLA Modules:
  0.0 60.5 jit_solution(8165620502957929640)
XLA Ops:
  0.6 55.3 %box_steps.1 = (f32[3,8,16,128]{3,2,1,0:T(8,128)}, f32[30,8,16,128]{3,2,1,0:T(8,128)}) custom-call(f32[3,8,16,128]{3,2,1,0:T(8,128)} %disp.1, f32[3,8,16,128]{3,2,1,0:T(8,128)} %velo.1, f32[30,8,16,128]{3,2,1,0:T(8,128)} %plas.1, f32[8,16,128]{2,1,0:T(8,128)} %mass.1, s32[8,16,128]{2,1,0:T(8,128)} %mate.1, f32[8,6]{1,0:T(8,128)} %moduli.1, f32[8,5]{1,0:T(8,128)} %radii.1, ...), custom_call_target="tpu_custom_call" | custom-call | tf_op jit(solution)/shard_map/box_steps/pallas_call | solution.py:485
  55.9 1.6 %copy.14 = f32[3,8,16,128]{3,2,1,0:T(8,128)} copy(f32[3,8,16,128]{3,2,1,0:T(8,128)} %get-tuple-element.4) | data formatting | bytes 393216
  57.5 3.0 %copy.15 = f32[30,8,16,128]{3,2,1,0:T(8,128)} copy(f32[30,8,16,128]{3,2,1,0:T(8,128)} %get-tuple-element.5) | data formatting | bytes 3932160

commit v3 on v2

--- a/solution.py
+++ b/solution.py
@@ -154,36 +154,6 @@
 
     lax.fori_loop(0, STEPS, own_forces, 0)
 
-    loads[3].wait()
-
-    def pack_rows(x, carry):
-        for c in range(3):
-            V[0, c, pl.ds(8 + x, 1), :] = U[1, c, x + 1, 0:1, :]
-            YH[0, c, pl.ds(x, 1), :] = U[1, c, x + 1, EY - 1 : EY, :]
-        return carry
-
-    lax.fori_loop(0, EX, pack_rows, 0)
-
-    def pack_corners(n):
-        CS[n, 0] = V[n, :, 8:9, :]
-        CS[n, 1] = YH[n, :, 0:1, :]
-        CS[n, 2] = V[n, :, 15:16, :]
-        CS[n, 3] = YH[n, :, 7:8, :]
-
-    pack_corners(0)
-
-    loads[4].wait()
-    PL[6 * SURF, 1 : EX + 1] = matev[...].astype(F32)
-    loads[2].wait()
-
-    def pack_plastic(k, carry):
-        for x in range(EX):
-            PYS[k, x : x + 1, :] = PL[k, x + 1, EY - 1 : EY, :]
-        PCS[k] = PYS[k, EX - 1 : EX, :]
-        return carry
-
-    lax.fori_loop(0, 6 * SURF + 1, pack_plastic, 0)
-
     pl.semaphore_wait(barrier, nx - 1 + 6)
 
     def remote(src, dst, send, recv, place):
@@ -224,6 +194,23 @@
             for i, (src, dst, place) in enumerate(pairs)
         ]
 
+    low_x, high_x, low_y, high_y = gx > 0, gx < nx - 1, gy > 0, gy < ny - 1
+    leaves = (
+        low_x, high_x, low_y, high_y,
+        low_x & low_y, low_x & high_y, high_x & low_y, high_x & high_y,
+    )
+    reaches = (
+        high_x, low_x, high_y, low_y,
+        high_x & high_y, high_x & low_y, low_x & high_y, low_x & low_y,
+    )
+
+    def where_true(copies, flags, act):
+        for copy, flag in zip(copies, flags):
+
+            @pl.when(flag)
+            def _(copy=copy):
+                act(copy)
+
     def plastic_halo():
         pairs = (
             (PL.at[:, EX], PL.at[:, 0], (xn, gy)),
@@ -235,9 +222,38 @@
             for i, (src, dst, place) in enumerate(pairs)
         ]
 
-    for copy in halo(0):
-        copy.start()
     send_forces(0)
+
+    loads[3].wait()
+
+    def pack_rows(x, carry):
+        for c in range(3):
+            V[0, c, pl.ds(8 + x, 1), :] = U[1, c, x + 1, 0:1, :]
+            YH[0, c, pl.ds(x, 1), :] = U[1, c, x + 1, EY - 1 : EY, :]
+        return carry
+
+    lax.fori_loop(0, EX, pack_rows, 0)
+
+    def pack_corners(n):
+        CS[n, 0] = V[n, :, 8:9, :]
+        CS[n, 1] = YH[n, :, 0:1, :]
+        CS[n, 2] = V[n, :, 15:16, :]
+        CS[n, 3] = YH[n, :, 7:8, :]
+
+    pack_corners(0)
+    where_true(halo(0), leaves, lambda copy: copy.start())
+
+    loads[4].wait()
+    PL[6 * SURF, 1 : EX + 1] = matev[...].astype(F32)
+    loads[2].wait()
+
+    def pack_plastic(k, carry):
+        for x in range(EX):
+            PYS[k, x : x + 1, :] = PL[k, x + 1, EY - 1 : EY, :]
+        PCS[k] = PYS[k, EX - 1 : EX, :]
+        return carry
+
+    lax.fori_loop(0, 6 * SURF + 1, pack_plastic, 0)
     for copy in plastic_halo():
         copy.start()
     send_forces(1)
@@ -315,8 +331,7 @@
                 PRY[k] = value * live if k <= SURF else value
 
         copies = halo(n)
-        for copy in copies:
-            copy.wait_recv()
+        where_true(copies, reaches, lambda copy: copy.wait_recv())
 
         def unpack(x, inner):
             for c in range(3):
@@ -328,6 +343,15 @@
         W[n, :, 16:17, :] = CR[n, 1]
         U[n + 1, :, 0, EY : EY + 1, :] = CR[n, 2]
         W[n, :, 7:8, :] = CR[n, 3]
+
+        @pl.when(gx == 0)
+        def _():
+            U[n + 1, :, 0] = jnp.zeros((3, EY + 8, NZ), F32)
+            W[n, :, 0:8, :] = jnp.zeros((3, 8, NZ), F32)
+
+        @pl.when(gy == 0)
+        def _():
+            W[n] = jnp.zeros((3, 24, NZ), F32)
 
         @pl.when(gx == nx - 1)
         def _():
@@ -421,15 +445,13 @@
         @pl.when(n < STEPS - 1)
         def _():
             pack_corners(n + 1)
-            for copy in halo(n + 1):
-                copy.start()
+            where_true(halo(n + 1), leaves, lambda copy: copy.start())
 
         @pl.when(n < STEPS - 2)
         def _():
             send_forces(n + 2)
 
-        for copy in copies:
-            copy.wait_send()
+        where_true(copies, leaves, lambda copy: copy.wait_send())
         return carry
 
     lax.fori_loop(0, STEPS, step, 0)
@@ -485,8 +507,8 @@
     return pl.pallas_call(
         functools.partial(kernel, nx, ny),
         out_shape=(
-            jax.ShapeDtypeStruct((3, EX, EY, NZ), F32),
-            jax.ShapeDtypeStruct((6 * SURF, EX, EY, NZ), F32),
+            pltpu.VMEM((3, EX, EY, NZ), F32),
+            pltpu.VMEM((6 * SURF, EX, EY, NZ), F32),
         ),
         in_specs=[any_space] * 5 + [smem] * 2 + [any_space] * 3,
         out_specs=(any_space, any_space),

time: 60.7 us -> 52.3 us (0.86)
  the two profiles are of different devices: /device:TPU:1 before, /device:TPU:3 now
where the time goes in v3:
time: 52.3 us; the launch traced here: 51.7 us
  Pallas kernels  49.1 us (94%)
  local copies, waits for them, and re-layouts  1.95 us (4%)
  between operations  0.64 us (1%)
    pallas_call x1, Pallas kernels, per_device(): pl.pallas_call(functools.partial(kernel, nx, ny), out_shape=(pltpu.VMEM((...  49.1 us
    unnamed x2, local copies, waits for them, and re-layouts  1.95 us

profile of v3, /device:TPU:3, one launch (start us, length us, event | category | flops | bytes accessed | tf_op | source)
XLA Modules:
  0.0 51.7 jit_solution(15375861373834049840)
XLA Ops:
  0.6 49.1 %box_steps.1 = (f32[3,8,16,128]{3,2,1,0:T(8,128)S(1)}, f32[30,8,16,128]{3,2,1,0:T(8,128)S(1)}) custom-call(f32[3,8,16,128]{3,2,1,0:T(8,128)} %disp.1, f32[3,8,16,128]{3,2,1,0:T(8,128)} %velo.1, f32[30,8,16,128]{3,2,1,0:T(8,128)} %plas.1, f32[8,16,128]{2,1,0:T(8,128)} %mass.1, s32[8,16,128]{2,1,0:T(8,128)} %mate.1, f32[8,6]{1,0:T(8,128)} %moduli.1, ...), custom_call_target="tpu_custom_call" | custom-call | tf_op jit(solution)/shard_map/box_steps/pallas_call | solution.py:507
  49.8 0.7 %copy.14 = f32[3,8,16,128]{3,2,1,0:T(8,128)} copy(f32[3,8,16,128]{3,2,1,0:T(8,128)S(1)} %get-tuple-element.2) | data formatting | bytes 393216
  50.4 1.3 %copy.15 = f32[30,8,16,128]{3,2,1,0:T(8,128)} copy(f32[30,8,16,128]{3,2,1,0:T(8,128)S(1)} %get-tuple-element.3) | data formatting | bytes 3932160

commit v4 on v3

--- a/solution.py
+++ b/solution.py
@@ -164,11 +164,11 @@
 
     def send_forces(n):
         def one(k, carry):
-            to = lax.rem(gx + k, nx)
+            to = jnp.where(gx + k < nx, gx + k, gx + k - nx)
             remote(FS.at[n, to], FR.at[n, gx], a_send.at[n], a_recv.at[n], (to, gy)).start()
             return carry
 
-        lax.fori_loop(1, nx, one, 0)
+        lax.fori_loop(1, nx, one, 0, unroll=nx - 1)
 
     def forces_done(n):
         some = FR.at[n, pl.ds(0, nx - 1)]
@@ -257,6 +257,7 @@
     for copy in plastic_halo():
         copy.start()
     send_forces(1)
+    send_forces(2)
 
     loads[5].wait()
 
@@ -311,9 +312,30 @@
         pltpu.make_async_copy(PL.at[pl.ds(0, 6 * SURF), pl.ds(1, EX)], out_plas, osem.at[1]),
     ]
 
+    def element(n, x, t):
+        lo = pl.ds(t * 8, 8)
+        up = pl.ds(t * 8 + 1, 8)
+        near = [(U[n + 1, c, x, lo, :], U[n + 1, c, x, up, :]) for c in range(3)]
+        far = [(U[n + 1, c, x + 1, lo, :], U[n + 1, c, x + 1, up, :]) for c in range(3)]
+        trace, dev = strains(near, far)
+
+        def write(k, value):
+            PL[k, x, lo, :] = value
+
+        sigma = stresses(
+            trace, dev, lambda k: PL[k, x, lo, :], write, lambda k: PR[k, x, lo, :]
+        )
+        for k in range(6):
+            SIG[k, x, t * 8 + 8 : t * 8 + 16, :] = sigma[k]
+
     def step(n, carry):
         for copy in forces_done(n):
             copy.wait()
+        def inside(x, inner):
+            element(n, x, 0)
+            return inner
+
+        lax.fori_loop(1, EX, inside, 0, unroll=EX - 1)
         scatter(n)
 
         @pl.when(n == 0)
@@ -383,25 +405,13 @@
                     for x in range(EX):
                         SIG[k, x + 1, 7:8, :] = sigma[k][x : x + 1, :]
 
-        def elements(x, inner):
-            for t in range(2):
-                lo = pl.ds(t * 8, 8)
-                up = pl.ds(t * 8 + 1, 8)
-                near = [(U[n + 1, c, x, lo, :], U[n + 1, c, x, up, :]) for c in range(3)]
-                far = [(U[n + 1, c, x + 1, lo, :], U[n + 1, c, x + 1, up, :]) for c in range(3)]
-                trace, dev = strains(near, far)
-
-                def write(k, value):
-                    PL[k, x, lo, :] = value
-
-                sigma = stresses(
-                    trace, dev, lambda k: PL[k, x, lo, :], write, lambda k: PR[k, x, lo, :]
-                )
-                for k in range(6):
-                    SIG[k, x, t * 8 + 8 : t * 8 + 16, :] = sigma[k]
+        def outside(x, inner):
+            element(n, x, 1)
             return inner
 
-        lax.fori_loop(0, EX + 1, elements, 0, unroll=EX + 1)
+        element(n, 0, 0)
+        element(n, EX, 0)
+        lax.fori_loop(0, EX + 1, outside, 0, unroll=EX + 1)
 
         @pl.when(n == STEPS - 1)
         def _():
@@ -447,9 +457,9 @@
             pack_corners(n + 1)
             where_true(halo(n + 1), leaves, lambda copy: copy.start())
 
-        @pl.when(n < STEPS - 2)
-        def _():
-            send_forces(n + 2)
+        @pl.when(n < STEPS - 3)
+        def _():
+            send_forces(n + 3)
 
         where_true(copies, leaves, lambda copy: copy.wait_send())
         return carry

time: 52.3 us -> 50.5 us (0.966)
  Pallas kernels: 49.1 us -> 47.7 us
    pallas_call x1, Pallas kernels: 49.1 us -> 47.7 us  [per_device(): pl.pallas_call(functools.partial(kernel, nx, ny), out_shape=(pltpu.VMEM((...]
where the time goes in v4:
time: 50.5 us; the launch traced here: 50.3 us
  Pallas kernels  47.7 us (94%)
  local copies, waits for them, and re-layouts  1.95 us (4%)
  between operations  0.64 us (1%)
    pallas_call x1, Pallas kernels, per_device(): pl.pallas_call(functools.partial(kernel, nx, ny), out_shape=(pltpu.VMEM((...  47.7 us
    unnamed x2, local copies, waits for them, and re-layouts  1.95 us

profile of v4, /device:TPU:3, one launch (start us, length us, event | category | flops | bytes accessed | tf_op | source)
XLA Modules:
  0.0 50.3 jit_solution(15884701252671332753)
XLA Ops:
  0.6 47.7 %box_steps.1 = (f32[3,8,16,128]{3,2,1,0:T(8,128)S(1)}, f32[30,8,16,128]{3,2,1,0:T(8,128)S(1)}) custom-call(f32[3,8,16,128]{3,2,1,0:T(8,128)} %disp.1, f32[3,8,16,128]{3,2,1,0:T(8,128)} %velo.1, f32[30,8,16,128]{3,2,1,0:T(8,128)} %plas.1, f32[8,16,128]{2,1,0:T(8,128)} %mass.1, s32[8,16,128]{2,1,0:T(8,128)} %mate.1, f32[8,6]{1,0:T(8,128)} %moduli.1, ...), custom_call_target="tpu_custom_call" | custom-call | tf_op jit(solution)/shard_map/box_steps/pallas_call | solution.py:517
  48.3 0.7 %copy.14 = f32[3,8,16,128]{3,2,1,0:T(8,128)} copy(f32[3,8,16,128]{3,2,1,0:T(8,128)S(1)} %get-tuple-element.2) | data formatting | bytes 393216
  49.0 1.3 %copy.15 = f32[30,8,16,128]{3,2,1,0:T(8,128)} copy(f32[30,8,16,128]{3,2,1,0:T(8,128)S(1)} %get-tuple-element.3) | data formatting | bytes 3932160

commit v5 on v4

--- a/solution.py
+++ b/solution.py
@@ -309,7 +309,19 @@
         pltpu.make_async_copy(
             U.at[STEPS + 1, :, pl.ds(1, EX), pl.ds(0, EY)], out_disp, osem.at[0]
         ),
-        pltpu.make_async_copy(PL.at[pl.ds(0, 6 * SURF), pl.ds(1, EX)], out_plas, osem.at[1]),
+        pltpu.make_async_copy(
+            PL.at[pl.ds(0, 6 * SURF), pl.ds(1, EX - 1), pl.ds(0, 8)],
+            out_plas.at[:, pl.ds(0, EX - 1), pl.ds(0, 8)],
+            osem.at[1],
+        ),
+        pltpu.make_async_copy(
+            PL.at[pl.ds(0, 6 * SURF), pl.ds(1, EX - 1), pl.ds(8, 8)],
+            out_plas.at[:, pl.ds(0, EX - 1), pl.ds(8, 8)],
+            osem.at[2],
+        ),
+        pltpu.make_async_copy(
+            PL.at[pl.ds(0, 6 * SURF), EX], out_plas.at[:, EX - 1], osem.at[3]
+        ),
     ]
 
     def element(n, x, t):
@@ -337,6 +349,11 @@
 
         lax.fori_loop(1, EX, inside, 0, unroll=EX - 1)
         scatter(n)
+
+        @pl.when(n == STEPS - 1)
+        def _():
+            outs[1].start()
+
 
         @pl.when(n == 0)
         def _():
@@ -415,7 +432,8 @@
 
         @pl.when(n == STEPS - 1)
         def _():
-            outs[1].start()
+            outs[2].start()
+            outs[3].start()
 
         def update(x, inner):
             for t in range(2):
@@ -506,7 +524,7 @@
         vmem((EX, EY, NZ), F32),
         vmem((EX, EY, NZ), jnp.int32),
         dma((8,)),
-        dma((2,)),
+        dma((4,)),
         dma((STEPS,)),
         dma((STEPS,)),
         dma((STEPS, 8)),

time: 50.5 us -> 50.5 us (level)
  no operation moved by 1% of the time
where the time goes in v5:
time: 50.5 us; the launch traced here: 50.3 us
  Pallas kernels  47.8 us (95%)
  local copies, waits for them, and re-layouts  1.95 us (4%)
  between operations  0.64 us (1%)
    pallas_call x1, Pallas kernels, per_device(): pl.pallas_call(functools.partial(kernel, nx, ny), out_shape=(pltpu.VMEM((...  47.8 us
    unnamed x2, local copies, waits for them, and re-layouts  1.95 us

profile of v5, /device:TPU:3, one launch (start us, length us, event | category | flops | bytes accessed | tf_op | source)
XLA Modules:
  0.0 50.3 jit_solution(13655870723965911137)
XLA Ops:
  0.6 47.8 %box_steps.1 = (f32[3,8,16,128]{3,2,1,0:T(8,128)S(1)}, f32[30,8,16,128]{3,2,1,0:T(8,128)S(1)}) custom-call(f32[3,8,16,128]{3,2,1,0:T(8,128)} %disp.1, f32[3,8,16,128]{3,2,1,0:T(8,128)} %velo.1, f32[30,8,16,128]{3,2,1,0:T(8,128)} %plas.1, f32[8,16,128]{2,1,0:T(8,128)} %mass.1, s32[8,16,128]{2,1,0:T(8,128)} %mate.1, f32[8,6]{1,0:T(8,128)} %moduli.1, ...), custom_call_target="tpu_custom_call" | custom-call | tf_op jit(solution)/shard_map/box_steps/pallas_call | solution.py:535
  48.4 0.7 %copy.14 = f32[3,8,16,128]{3,2,1,0:T(8,128)} copy(f32[3,8,16,128]{3,2,1,0:T(8,128)S(1)} %get-tuple-element.2) | data formatting | bytes 393216
  49.1 1.3 %copy.15 = f32[30,8,16,128]{3,2,1,0:T(8,128)} copy(f32[30,8,16,128]{3,2,1,0:T(8,128)S(1)} %get-tuple-element.3) | data formatting | bytes 3932160
